TPU v7x, 128 devices: a whole 4x4x4 slice. The times are simulated.
128 devices in a mesh: dp: 8 (over y_lo, z), tp: 16 (over y_hi, x, core).
Axes of the slice: x: 4, y: 4 (y_hi: 2, y_lo: 2; y = y_hi * 2 + y_lo), z: 4, core: 2. Of those that a mesh axis runs over, the one named last changes fastest.
Arguments:
- tokens: bfloat16 [4096, 2304], P(('dp', 'tp')), may hold values from -36 to 36
- gain_pre: float32 [2304], replicated, may hold values from 0.1 to 1.9
- gain_post: float32 [2304], replicated, may hold values from 0.1 to 1.9
- gate_weight: bfloat16 [2304, 18432], P(None, 'tp'), may hold values from -0.125 to 0.125
- up_weight: bfloat16 [2304, 18432], P(None, 'tp'), may hold values from -0.125 to 0.125
- down_weight: bfloat16 [18432, 2304], P('tp'), may hold values from -0.046875 to 0.046875
- cotangent: bfloat16 [4096, 2304], P(('dp', 'tp')), may hold values from -1.5 to 1.5
Outputs:
- block_out: bfloat16 [4096, 2304], P(('dp', 'tp'))
- tokens_grad: bfloat16 [4096, 2304], P(('dp', 'tp'))
- gain_pre_grad: float32 [2304], replicated
- gain_post_grad: float32 [2304], replicated
- gate_grad: float32 [2304, 18432], P('dp', 'tp')
- up_grad: float32 [2304, 18432], P('dp', 'tp')
- down_grad: float32 [18432, 2304], P(('tp', 'dp'))
All inputs are finite; a program needn't handle non-finite values.
Results may differ from a plain program's by a relative error of at most 0.02.
Values may be sent and summed in bfloat16 or wider, within the bound.
A program may use at most 128 MiB of HBM per device.

v0:
```python
import jax
import jax.numpy as jnp
from jax import lax
from jax.sharding import PartitionSpec as P

epsilon = 1e-06
root_two_pi = 0.7978845608028654


def gelu_pair(values):
    tanh_arg = root_two_pi * (values + 0.044715 * values * values * values)
    hyper = jnp.tanh(tanh_arg)
    gelu_value = 0.5 * values * (1.0 + hyper)
    gelu_slope = 0.5 * (1.0 + hyper) + 0.5 * values * (1.0 - hyper * hyper) * root_two_pi * (
        1.0 + 3.0 * 0.044715 * values * values
    )
    return (gelu_value, gelu_slope)


def norm_parts(values):
    recip = lax.rsqrt(jnp.mean(values * values, axis=-1, keepdims=True) + epsilon)
    return (values * recip, recip)


def norm_back(grad_in, scaled, recip, gain):
    weighted = grad_in * gain
    return recip * (weighted - scaled * jnp.mean(weighted * scaled, axis=-1, keepdims=True))


def contract_rows(left_side, right_side):
    return lax.dot_general(
        left_side, right_side, (((0,), (0,)), ((), ())), preferred_element_type=jnp.float32
    )


def contract_cols(left_side, right_side):
    return lax.dot_general(
        left_side, right_side, (((1,), (1,)), ((), ())), preferred_element_type=jnp.float32
    )


def local(tokens, gain_pre, gain_post, gate_weight, up_weight, down_weight, cotangent):
    inputs_f = tokens.astype(jnp.float32)
    scaled_in, recip_in = norm_parts(inputs_f)
    normed = (scaled_in * gain_pre).astype(jnp.bfloat16)
    ff_width = gate_weight.shape[1]
    shard_piece = lax.all_gather(normed, "tp", axis=0, tiled=True)
    gate_part = jnp.dot(shard_piece, gate_weight, preferred_element_type=jnp.float32)
    up_part = jnp.dot(shard_piece, up_weight, preferred_element_type=jnp.float32)
    joined = jnp.concatenate([gate_part, up_part], axis=1)
    gate_pre = joined[:, :ff_width]
    up_pre = joined[:, ff_width:]
    activated, gelu_slope = gelu_pair(gate_pre)
    hidden = (activated * up_pre).astype(jnp.bfloat16)
    mixed = lax.psum_scatter(
        jnp.dot(hidden, down_weight, preferred_element_type=jnp.float32).astype(jnp.bfloat16),
        "tp",
        scatter_dimension=0,
        tiled=True,
    ).astype(jnp.float32)
    scaled_mix, recip_mix = norm_parts(mixed)
    block_out = (inputs_f + scaled_mix * gain_post).astype(jnp.bfloat16)
    cot_f = cotangent.astype(jnp.float32)
    post_term = jnp.sum(cot_f * scaled_mix, axis=0)
    mix_grad = norm_back(cot_f, scaled_mix, recip_mix, gain_post).astype(jnp.bfloat16)
    shard_piece = lax.all_gather(mix_grad, "tp", axis=0, tiled=True)
    hidden_acc = contract_cols(shard_piece, down_weight)
    down_local = contract_rows(hidden, shard_piece)
    up_pre_grad = (hidden_acc * activated).astype(jnp.bfloat16)
    gate_pre_grad = (hidden_acc * up_pre * gelu_slope).astype(jnp.bfloat16)
    collected = lax.all_gather(normed, "tp", axis=0, tiled=True)
    gate_local = contract_rows(collected, gate_pre_grad)
    up_local = contract_rows(collected, up_pre_grad)
    normed_grad = lax.psum_scatter(
        (contract_cols(gate_pre_grad, gate_weight) + contract_cols(up_pre_grad, up_weight)).astype(
            jnp.bfloat16
        ),
        "tp",
        scatter_dimension=0,
        tiled=True,
    ).astype(jnp.float32)
    gate_grad, up_grad, down_grad = (
        lax.psum_scatter(
            gate_local.astype(jnp.bfloat16), "dp", scatter_dimension=0, tiled=True
        ).astype(jnp.float32),
        lax.psum_scatter(
            up_local.astype(jnp.bfloat16), "dp", scatter_dimension=0, tiled=True
        ).astype(jnp.float32),
        lax.psum_scatter(
            down_local.astype(jnp.bfloat16), "dp", scatter_dimension=0, tiled=True
        ).astype(jnp.float32),
    )
    pre_term = jnp.sum(normed_grad * scaled_in, axis=0)
    tokens_grad = (cot_f + norm_back(normed_grad, scaled_in, recip_in, gain_pre)).astype(
        jnp.bfloat16
    )
    gain_pre_grad, gain_post_grad = lax.psum((pre_term, post_term), ("dp", "tp"))
    return (block_out, tokens_grad, gain_pre_grad, gain_post_grad, gate_grad, up_grad, down_grad)


def solution(mesh):
    in_specs = (
        P(("dp", "tp"), None),
        P(),
        P(),
        P(None, "tp"),
        P(None, "tp"),
        P("tp", None),
        P(("dp", "tp"), None),
    )
    out_specs = (
        P(("dp", "tp"), None),
        P(("dp", "tp"), None),
        P(),
        P(),
        P("dp", "tp"),
        P("dp", "tp"),
        P(("tp", "dp"), None),
    )
    return jax.shard_map(local, mesh=mesh, in_specs=in_specs, out_specs=out_specs, check_vma=False)
```

profile of v0, /device:TPU:1, one launch (start us, length us, event | category | flops | bytes accessed | tf_op | source)
XLA Modules:
  0.0 512.9 jit_solution(8619260118680380730)
XLA Ops:
  7.2 0.0 all-gather.3.cloned.1.call-start
  7.2 1.0 fusion.25
  8.3 1.7 fusion.22
  10.0 0.0 all-gather.3.cloned.1.call-update
  10.0 0.0 reduce-scatter.6.cloned.1.call-start
  10.0 54.0 %all-gather.3.cloned.1.call-done = bf16[512,2304]{1,0:T(8,128)(2,1)} async-done(((bf16[32,2304]{1,0:T(8,128)(2,1)}), bf16[512,2304]{1,0:T(8,128)(2,1)}) %all-gather.3.cloned.1.call-update) | async-done | bytes 2359312 | tf_op jit(solution)/shard_map/all_gather | solution.py:47
  64.0 0.0 copy-start.5
  64.1 6.6 %fusion.29 = f32[512,1152]{1,0:T(8,128)S(1)} fusion(bf16[512,2304]{1,0:T(8,128)(2,1)} %all-gather.3.cloned.1.call-done, bf16[2304,1152]{1,0:T(8,128)(2,1)} %param.10), kind=kOutput, calls=%fused_computation.52 | convolution fusion | flops 2717908992 | bytes 10027008 | tf_op jit(solution)/shard_map/dot_general | solution.py:48
  70.6 0.0 copy-done.5
  70.6 0.0 copy-start.6
  70.6 0.0 copy-start.4
  70.7 8.2 %multiply_convert_fusion.1 = (bf16[512,1152]{1,0:T(8,128)(2,1)S(1)}, f32[512,1152]{1,0:T(8,128)}) fusion(f32[512,1152]{1,0:T(8,128)S(1)} %fusion.29, bf16[512,2304]{1,0:T(8,128)(2,1)S(1)} %copy-done.5, bf16[2304,1152]{1,0:T(8,128)(2,1)} %param.11), kind=kOutput, calls=%fused_computation.16 | convolution fusion | flops 2723807232 | bytes 13565952 | tf_op jit(solution)/shard_map/dot_general | solution.py:49
  78.9 0.0 copy-done.6
  78.9 0.0 copy-start.7
  78.9 1.0 copy-done.7
  79.9 0.0 copy-done.4
  79.9 4.4 convolution_convert_fusion.3
  84.3 0.0 copy-start.1
  84.3 0.0 copy-start.3
  84.3 0.0 copy-start
  84.3 0.0 reduce-scatter.6.cloned.1.call-update
  84.3 0.0 all-gather.5.cloned.1.call-start
  84.4 68.8 %reduce-scatter.6.cloned.1.call-done = bf16[32,2304]{1,0:T(8,128)(2,1)} async-done(((bf16[512,2304]{1,0:T(8,128)(2,1)}), bf16[32,2304]{1,0:T(8,128)(2,1)}) %reduce-scatter.6.cloned.1.call-update) | async-done | bytes 147472 | tf_op jit(solution)/shard_map/reduce_scatter | solution.py:55
  153.2 1.0 fusion.21
  154.3 0.0 copy-done.1
  154.3 0.0 copy-done.3
  154.3 1.2 fusion.28
  155.5 0.0 copy-done
  155.5 1.8 fusion.18
  157.3 0.0 all-gather.5.cloned.1.call-update
  157.3 0.2 reduce-scatter.8.cloned.1.call-start
  157.5 50.7 %all-gather.5.cloned.1.call-done = bf16[512,2304]{1,0:T(8,128)(2,1)} async-done(((bf16[32,2304]{1,0:T(8,128)(2,1)}), bf16[512,2304]{1,0:T(8,128)(2,1)}) %all-gather.5.cloned.1.call-update) | async-done | bytes 2359312 | tf_op jit(solution)/shard_map/all_gather | solution.py:66
  208.2 8.9 %multiply_convert_fusion = (bf16[512,1152]{1,0:T(8,128)(2,1)S(1)}, bf16[512,1152]{1,0:T(8,128)(2,1)S(1)}) fusion(f32[512,1152]{1,0:T(8,128)} %copy-done.6, f32[512,1152]{1,0:T(8,128)} %get-tuple-element.18, bf16[512,2304]{1,0:T(8,128)(2,1)} %all-gather.5.cloned.1.call-done, bf16[1152,2304]{1,0:T(8,128)(2,1)} %param.12), kind=kOutput, calls=%fused_computation.15 | convolution fusion | flops 2731474944 | bytes 14745600 | tf_op jit(solution)/shard_map/dot_general | solution.py:37
  217.1 0.0 copy-start.9
  217.2 0.0 copy-start.8
  217.2 6.6 %fusion.30 = f32[512,2304]{1,0:T(8,128)S(1)} fusion(bf16[512,1152]{1,0:T(8,128)(2,1)S(1)} %get-tuple-element.14, bf16[2304,1152]{1,0:T(8,128)(2,1)} %param.10), kind=kOutput, calls=%fused_computation.53 | convolution fusion | flops 2717908992 | bytes 11206656 | tf_op jit(solution)/shard_map/dot_general | solution.py:37
  223.8 0.0 copy-done.9
  223.8 0.0 copy-done.8
  223.8 7.0 %fusion = bf16[512,2304]{1,0:T(8,128)(2,1)} fusion(f32[512,2304]{1,0:T(8,128)S(1)} %fusion.30, bf16[512,1152]{1,0:T(8,128)(2,1)S(1)} %get-tuple-element.13, bf16[2304,1152]{1,0:T(8,128)(2,1)} %param.11), kind=kOutput, calls=%fused_computation.5 | convolution fusion | flops 2720268288 | bytes 13565952 | tf_op jit(solution)/shard_map/dot_general | solution.py:37
  230.8 0.0 reduce-scatter.8.cloned.1.call-update
  230.9 0.0 reduce-scatter.14.cloned.1.call-start
  230.9 7.3 %convolution_convert_fusion = bf16[1152,2304]{1,0:T(8,128)(2,1)} fusion(bf16[512,1152]{1,0:T(8,128)(2,1)} %copy-done.7, bf16[512,2304]{1,0:T(8,128)(2,1)} %all-gather.5.cloned.1.call-done), kind=kOutput, calls=%fused_computation | convolution fusion | flops 2720563200 | bytes 8847360 | tf_op jit(solution)/shard_map/dot_general | solution.py:31
  238.2 0.0 reduce-scatter.14.cloned.1.call-update
  238.2 0.0 reduce-scatter.12.cloned.1.call-start
  238.3 6.3 %convolution_convert_fusion.1 = bf16[2304,1152]{1,0:T(8,128)(2,1)} fusion(bf16[512,2304]{1,0:T(8,128)(2,1)S(1)} %copy-done.5, bf16[512,1152]{1,0:T(8,128)(2,1)} %copy-done.8), kind=kOutput, calls=%fused_computation.1 | convolution fusion | flops 2720563200 | bytes 8847360 | tf_op jit(solution)/shard_map/dot_general | solution.py:31
  244.6 0.0 reduce-scatter.12.cloned.1.call-update
  244.6 0.3 reduce-scatter.10.cloned.1.call-start
  244.9 6.4 %convolution_convert_fusion.2 = bf16[2304,1152]{1,0:T(8,128)(2,1)} fusion(bf16[512,2304]{1,0:T(8,128)(2,1)S(1)} %copy-done.5, bf16[512,1152]{1,0:T(8,128)(2,1)} %copy-done.9), kind=kOutput, calls=%fused_computation.2 | convolution fusion | flops 2720563200 | bytes 8847360 | tf_op jit(solution)/shard_map/dot_general | solution.py:31
  251.2 0.0 copy-start.2
  251.2 0.0 reduce-scatter.10.cloned.1.call-update
  251.3 48.5 %reduce-scatter.8.cloned.1.call-done = bf16[32,2304]{1,0:T(8,128)(2,1)} async-done(((bf16[512,2304]{1,0:T(8,128)(2,1)}), bf16[32,2304]{1,0:T(8,128)(2,1)}) %reduce-scatter.8.cloned.1.call-update) | async-done | bytes 147472 | tf_op jit(solution)/shard_map/reduce_scatter | solution.py:74
  299.8 0.0 copy-done.2
  299.8 1.2 fusion.24
  301.0 196.6 %all-reduce = (f32[2304]{0:T(1024)}, f32[2304]{0:T(1024)}) all-reduce(f32[2304]{0:T(1024)S(1)} %get-tuple-element.9, f32[2304]{0:T(1024)S(1)} %get-tuple-element.7), channel_id=1, replica_groups=mesh['dp'=8,'tp'=16] {'dp','tp'}, use_global_device_ids=true, to_apply=%region_7.0 | all-reduce | flops 4608 | bytes 36864 | tf_op jit(solution)/shard_map/psum | solution.py:97
  497.6 1.7 fusion.27
  499.3 0.0 reduce-scatter.14.cloned.1.call-done
  499.3 2.2 convert_element_type.75
  501.5 0.0 reduce-scatter.12.cloned.1.call-done
  501.5 2.2 convert_element_type.73
  503.8 0.0 reduce-scatter.10.cloned.1.call-done
  503.8 2.2 convert_element_type.71
  (4 shorter events, 0.0 us)
Async XLA Ops:
  7.2 56.9 %all-gather.3.cloned.1.call-start = ((), (), s32[]{:S(2)}) async-start(), calls=%async_computation.5 | async-start | bytes 2506752 | tf_op jit(solution)/shard_map/all_gather | solution.py:47
  10.0 143.2 %reduce-scatter.6.cloned.1.call-start = ((), (), s32[]{:S(2)}) async-start(), calls=%async_computation.6 | async-start | bytes 2506752 | tf_op jit(solution)/shard_map/reduce_scatter | solution.py:55
  64.0 6.6 %copy-start.5 = (bf16[512,2304]{1,0:T(8,128)(2,1)S(1)}, bf16[512,2304]{1,0:T(8,128)(2,1)}, u32[]{:S(2)}) copy-start(bf16[512,2304]{1,0:T(8,128)(2,1)} %all-gather.3.cloned.1.call-done) | copy-start | bytes 7077892
  70.6 8.3 %copy-start.6 = (f32[512,1152]{1,0:T(8,128)}, f32[512,1152]{1,0:T(8,128)S(1)}, u32[]{:S(2)}) copy-start(f32[512,1152]{1,0:T(8,128)S(1)} %fusion.29) | copy-start | bytes 7077892
  70.6 9.3 %copy-start.4 = (bf16[1152,2304]{1,0:T(8,128)(2,1)S(1)}, bf16[1152,2304]{1,0:T(8,128)(2,1)}, u32[]{:S(2)}) copy-start(bf16[1152,2304]{1,0:T(8,128)(2,1)} %param.12) | copy-start | bytes 15925252
  78.9 1.0 copy-start.7
  84.3 70.0 %copy-start.1 = (bf16[32,2304]{1,0:T(8,128)(2,1)S(1)}, bf16[32,2304]{1,0:T(8,128)(2,1)}, u32[]{:S(2)}) copy-start(bf16[32,2304]{1,0:T(8,128)(2,1)} %param.13) | copy-start | bytes 442372
  84.3 70.0 %copy-start.3 = (f32[2304]{0:T(1024)S(1)}, f32[2304]{0:T(1024)}, u32[]{:S(2)}) copy-start(f32[2304]{0:T(1024)} %param.9) | copy-start | bytes 27652
  84.3 71.2 %copy-start = (bf16[32,2304]{1,0:T(8,128)(2,1)S(1)}, bf16[32,2304]{1,0:T(8,128)(2,1)}, u32[]{:S(2)}) copy-start(bf16[32,2304]{1,0:T(8,128)(2,1)} %param.7) | copy-start | bytes 442372
  84.3 123.9 %all-gather.5.cloned.1.call-start = ((), (), s32[]{:S(2)}) async-start(), calls=%async_computation.7 | async-start | bytes 2506752 | tf_op jit(solution)/shard_map/all_gather | solution.py:66
  157.3 142.5 %reduce-scatter.8.cloned.1.call-start = ((), (), s32[]{:S(2)}) async-start(), calls=%async_computation.8 | async-start | bytes 2506752 | tf_op jit(solution)/shard_map/reduce_scatter | solution.py:74
  217.1 6.7 %copy-start.9 = (bf16[512,1152]{1,0:T(8,128)(2,1)}, bf16[512,1152]{1,0:T(8,128)(2,1)S(1)}, u32[]{:S(2)}) copy-start(bf16[512,1152]{1,0:T(8,128)(2,1)S(1)} %get-tuple-element.14) | copy-start | bytes 3538948
  217.2 6.7 %copy-start.8 = (bf16[512,1152]{1,0:T(8,128)(2,1)}, bf16[512,1152]{1,0:T(8,128)(2,1)S(1)}, u32[]{:S(2)}) copy-start(bf16[512,1152]{1,0:T(8,128)(2,1)S(1)} %get-tuple-element.13) | copy-start | bytes 3538948
  230.9 268.4 %reduce-scatter.14.cloned.1.call-start = ((), (), s32[]{:S(2)}) async-start(), calls=%async_computation.11 | async-start | bytes 5971968 | tf_op jit(solution)/shard_map/reduce_scatter | solution.py:89
  238.2 263.3 %reduce-scatter.12.cloned.1.call-start = ((), (), s32[]{:S(2)}) async-start(), calls=%async_computation.10 | async-start | bytes 5971968 | tf_op jit(solution)/shard_map/reduce_scatter | solution.py:86
  244.6 259.2 %reduce-scatter.10.cloned.1.call-start = ((), (), s32[]{:S(2)}) async-start(), calls=%async_computation.9 | async-start | bytes 5971968 | tf_op jit(solution)/shard_map/reduce_scatter | solution.py:83
  251.2 48.6 %copy-start.2 = (f32[2304]{0:T(1024)S(1)}, f32[2304]{0:T(1024)}, u32[]{:S(2)}) copy-start(f32[2304]{0:T(1024)} %param.8) | copy-start | bytes 27652
Sparse Core Ops, SparseCore 0:
  11.0 53.0 all-gather.2
  84.5 68.7 reduce-scatter.5
  157.4 50.7 all-gather.4
  231.0 68.7 reduce-scatter.7
  302.1 65.1 reduce-scatter.13
  369.5 62.3 reduce-scatter.11
  434.4 62.8 reduce-scatter.9
where the time goes:
time: 514 us; the launch traced here: 513 us
  waiting for transfers between devices  222 us (43%)
  blocking collectives  197 us (38%)
  matrix products  61.7 us (12%)
  other arithmetic  16.3 us (3%)
  between operations  14.2 us (3%)
    psum x1, blocking collectives, local(): lax.psum((pre_term, post_term), ('dp', 'tp'))  197 us
    reduce_scatter x1, waiting for transfers between devices, local(): lax.psum_scatter(jnp.dot(hidden, down_weight, preferred_element_type=jnp....  68.8 us
    all_gather x1, waiting for transfers between devices, local(): shard_piece = lax.all_gather(normed, 'tp', axis=0, tiled=True)  54 us
    all_gather x1, waiting for transfers between devices, local(): shard_piece = lax.all_gather(mix_grad, 'tp', axis=0, tiled=True)  50.7 us
    reduce_scatter x1, waiting for transfers between devices, local(): lax.psum_scatter((contract_cols(gate_pre_grad, gate_weight) + contract_co...  48.5 us
    dot_general x3, matrix products, contract_cols(): lax.dot_general(left_side, right_side, (((1,), (1,)), ((), ())), preferre...  22.6 us
    dot_general x3, matrix products, contract_rows(): lax.dot_general(left_side, right_side, (((0,), (0,)), ((), ())), preferre...  20 us
  transfers between devices with their start and end apart: 7, of which 4 were waited for; matrix products, arithmetic and copies ran while one was open for 5% of the time, Pallas kernels for 0%

commit v1 on v0

v1 whole, which is shorter than its diff:
```python
import jax
import jax.numpy as jnp
from jax import lax
from jax.experimental import pallas as pl
from jax.experimental.pallas import tpu as pltpu
from jax.sharding import PartitionSpec as P

epsilon = 1e-06
root_two_pi = 0.7978845608028654
MESH = pl.DeviceIdType.MESH
D = 2304
F = 1152
B = 32
T = 384
f32 = jnp.float32
bf16 = jnp.bfloat16


def gelu_pair(values):
    tanh_arg = root_two_pi * (values + 0.044715 * values * values * values)
    hyper = jnp.tanh(tanh_arg)
    gelu_value = 0.5 * values * (1.0 + hyper)
    gelu_slope = 0.5 * (1.0 + hyper) + 0.5 * values * (1.0 - hyper * hyper) * root_two_pi * (
        1.0 + 3.0 * 0.044715 * values * values
    )
    return (gelu_value, gelu_slope)


def nt(a, b):
    return lax.dot_general(a, b, (((1,), (1,)), ((), ())), preferred_element_type=f32)


def nn(a, b):
    return jnp.dot(a, b, preferred_element_type=f32)


def tile(j, width=T):
    return pl.ds(pl.multiple_of(j * width, 128), width)


def kernel(
    tok, cot, gpre, gpost, wg_h, wu_h, wd_h,
    bout, tgrad, gain_pre_out, gain_post_out, d_own, d_a, d_b, g_own, g_a, g_b, u_own, u_a, u_b,
    wg, wu, wd, nbuf, mgbuf, act, us, hown, ht, ntr, part, crecv, xrecv, ysend, yrecv,
    zd, zg, zu, zdf, zgf, zuf, gv, gc, gx, gy, gz,
    wsem, ag1s, ag1r, ag2s, ag2r, rs1s, rs1r, rs2s, rs2r, zs, zr, zl, gs, gr,
):
    dp, tp = lax.axis_index("dp"), lax.axis_index("tp")
    c = tp % 2
    x = (tp // 2) % 4
    yh = tp // 8
    yl = dp // 4
    z = dp % 4
    y = yh * 2 + yl

    def dev(dx=0, dy=0, dz=0, dc=0):
        yy = (y + dy) % 4
        return ((yy % 2) * 4 + (z + dz) % 4, ((yy // 2) * 4 + (x + dx) % 4) * 2 + (c + dc) % 2)

    loads = [
        pltpu.make_async_copy(h, v, wsem.at[i])
        for i, (h, v) in enumerate(((wg_h, wg), (wu_h, wu), (wd_h, wd)))
    ]
    for load in loads:
        load.start()

    barrier = pltpu.get_barrier_semaphore()
    offs = [dict(dc=1)] + [{a: k} for a in ("dx", "dy", "dz") for k in (1, 2, 3)]
    for o in offs:
        pl.semaphore_signal(barrier, inc=1, device_id=dev(**o), device_id_type=MESH)

    def remote(src, dst, s, r, to):
        return pltpu.make_async_remote_copy(
            src_ref=src, dst_ref=dst, send_sem=s, recv_sem=r, device_id=to, device_id_type=MESH
        )

    def blk(buf, df, ds, core=None):
        dx = df * (1 - c) + ds * c
        dy = df * c + ds * (1 - c)
        xx, yy = (x + dx) % 4, (y + dy) % 4
        return buf.at[yy % 2, yy // 2, xx, c]

    def other_blk(buf, df, ds):
        dx = df * c + ds * (1 - c)
        dy = df * (1 - c) + ds * c
        xx, yy = (x + dx) % 4, (y + dy) % 4
        return buf.at[yy % 2, yy // 2, xx, 1 - c]

    def to_f(sign):
        return dev(dx=(1 - c) * (sign % 4), dy=c * (sign % 4))

    def to_s(sign):
        return dev(dx=c * (sign % 4), dy=(1 - c) * (sign % 4))

    def gather(buf, ss, rr):
        sent = []

        def send(i, ref, to):
            cp = remote(ref, ref, ss.at[i], rr.at[i], to)
            cp.start()
            sent.append(cp)

        def got(i, ref):
            remote(ref, ref, ss.at[i], rr.at[i], dev(dc=1)).wait_recv()

        def core(df, ds):
            send(16 + ds * 4 + df, blk(buf, df, ds), dev(dc=1))

        own = blk(buf, 0, 0)
        send(0, own, to_f(1))
        send(1, own, to_f(-1))
        send(4, own, to_s(1))
        send(8, own, to_s(-1))
        core(0, 0)
        got(0, blk(buf, 3, 0))
        send(2, blk(buf, 3, 0).at[pl.ds(0, 16)], to_f(1))
        send(7, blk(buf, 3, 0), to_s(1))
        send(11, blk(buf, 3, 0), to_s(-1))
        core(3, 0)
        got(1, blk(buf, 1, 0))
        send(3, blk(buf, 1, 0).at[pl.ds(16, 16)], to_f(-1))
        send(5, blk(buf, 1, 0), to_s(1))
        send(9, blk(buf, 1, 0), to_s(-1))
        core(1, 0)
        got(2, blk(buf, 2, 0).at[pl.ds(0, 16)])
        got(3, blk(buf, 2, 0).at[pl.ds(16, 16)])
        send(6, blk(buf, 2, 0), to_s(1))
        send(10, blk(buf, 2, 0), to_s(-1))
        core(2, 0)
        for df, fwd_a, fwd_b in ((0, 12, None), (1, 13, None), (3, None, 14), (2, None, 15)):
            got(4 + df, blk(buf, df, 3))
            if fwd_a is not None:
                send(fwd_a, blk(buf, df, 3), to_s(1))
            core(df, 3)
            got(8 + df, blk(buf, df, 1))
            if fwd_b is not None:
                send(fwd_b, blk(buf, df, 1), to_s(-1))
            core(df, 1)
        for i, df in ((12, 0), (13, 1), (14, 3), (15, 2)):
            got(i, blk(buf, df, 2))
            core(df, 2)
        for ds in range(4):
            for df in range(4):
                got(16 + ds * 4 + df, other_blk(buf, df, ds))
        return sent

    def core_send(half, i, ss, rr):
        cp = remote(part.at[half, :, 1 - c], crecv.at[i], ss.at[i], rr.at[i], dev(dc=1))
        cp.start()
        return cp

    def core_add(half, i, ss, rr):
        remote(crecv.at[i], crecv.at[i], ss.at[i], rr.at[i], dev(dc=1)).wait_recv()

        def one(k, _):
            part[half, k, c] = (part[half, k, c].astype(f32) + crecv[i, k].astype(f32)).astype(bf16)
            return 0

        lax.fori_loop(0, 4, one, 0)

    def x_send(half, i, ss, rr):
        out = []
        for dx in (2, 1, 3):
            k = 2 + i * 3 + dx - 1
            cp = remote(
                part.at[half, (x + dx) % 4, c], xrecv.at[i, dx - 1], ss.at[k], rr.at[k], dev(dx=dx)
            )
            cp.start()
            out.append(cp)
        return out

    def x_sum(half, i, ss, rr):
        for dx in (1, 3, 2):
            k = 2 + i * 3 + dx - 1
            ref = xrecv.at[i, dx - 1]
            remote(ref, ref, ss.at[k], rr.at[k], dev(dx=dx)).wait_recv()
        total = part[half, x, c].astype(f32)
        for dx in (1, 3, 2):
            total = total + xrecv[i, dx - 1].astype(f32)
        return total

    def y_send(total, ss, rr):
        ysend[...] = total.astype(bf16)
        cp = remote(ysend, yrecv, ss.at[8], rr.at[8], dev(dy=2))
        cp.start()
        return cp

    def y_sum(total, ss, rr):
        remote(yrecv, yrecv, ss.at[8], rr.at[8], dev(dy=2)).wait_recv()
        return total + yrecv[...].astype(f32)

    tok_f = tok[...].astype(f32)
    recip_in = lax.rsqrt(jnp.mean(tok_f * tok_f, axis=-1, keepdims=True) + epsilon)
    nbuf[yl, yh, x, c] = (tok_f * recip_in * gpre[...]).astype(bf16)

    pl.semaphore_wait(barrier, len(offs))
    sent1 = gather(nbuf, ag1s, ag1r)
    for load in loads:
        load.wait()

    def forward(yy, is_own):
        a, b = yy % 2, yy // 2
        k = a * 2 + b

        def one(j, _):
            rows = nbuf[a, b].reshape(256, D)
            gate = nn(rows, wg[:, tile(j)])
            up = nn(rows, wu[:, tile(j)])
            value, slope = gelu_pair(gate)
            hidden = (value * up).astype(bf16)
            act[a, b, :, tile(j)] = value.astype(bf16)
            us[a, b, :, tile(j)] = (up * slope).astype(bf16)
            if is_own:
                hown[b, :, tile(j)] = hidden
            ht[tile(j), tile(k, 256)] = hidden.T
            return 0

        lax.fori_loop(0, 3, one, 0)

    def down(half):
        def one(j, _):
            part[half, :, :, :, tile(j)] = (
                nn(hown[half], wd[:, tile(j)]).astype(bf16).reshape(4, 2, B, T)
            )
            return 0

        lax.fori_loop(0, 6, one, 0)

    forward((y + 2) % 4, True)
    down(1 - yh)
    pend = [core_send(1 - yh, 0, rs1s, rs1r)]
    forward(y, True)
    core_add(1 - yh, 0, rs1s, rs1r)
    pend += x_send(1 - yh, 0, rs1s, rs1r)
    down(yh)
    pend.append(core_send(yh, 1, rs1s, rs1r))
    core_add(yh, 1, rs1s, rs1r)
    pend += x_send(yh, 1, rs1s, rs1r)
    forward((y + 1) % 4, False)
    pend.append(y_send(x_sum(1 - yh, 0, rs1s, rs1r), rs1s, rs1r))
    forward((y + 3) % 4, False)
    mixed = y_sum(x_sum(yh, 1, rs1s, rs1r), rs1s, rs1r)

    recip_mix = lax.rsqrt(jnp.mean(mixed * mixed, axis=-1, keepdims=True) + epsilon)
    scaled_mix = mixed * recip_mix
    cot_f = cot[...].astype(f32)
    weighted = cot_f * gpost[...]
    mix_grad = recip_mix * (
        weighted - scaled_mix * jnp.mean(weighted * scaled_mix, axis=-1, keepdims=True)
    )
    mgbuf[yl, yh, x, c] = mix_grad.astype(bf16)
    bout[...] = (tok[...].astype(f32) + scaled_mix * gpost[...]).astype(bf16)
    gv[...] = jnp.zeros_like(gv)
    gv[1:2, :] = jnp.sum(cot_f * scaled_mix, axis=0, keepdims=True)
    for cp in pend + sent1:
        cp.wait_send()

    sent2 = gather(mgbuf, ag2s, ag2r)

    def turn(k, _):
        rows = nbuf[k // 2, k % 2].reshape(256, D)
        del rows

        def one(j, _):
            cols = pl.ds(pl.multiple_of(yl * F + j * T, 128), T)
            ntr[tile(j), tile(k, 256)] = nbuf[k // 2, k % 2, :, :, :, cols].reshape(256, T).T
            return 0

        lax.fori_loop(0, 3, one, 0)
        return 0

    lax.fori_loop(0, 4, turn, 0)

    units = {}
    sent3 = []

    def halves(ref, kind, k):
        if kind == "d":
            return ref.at[:, pl.ds(k * T, T)]
        return ref.at[pl.ds(k * 144, 144)]

    bufs = {"d": (zd, zdf, d_own, d_a, d_b, 0), "g": (zg, zgf, g_own, g_a, g_b, 3), "u": (zu, zuf, u_own, u_a, u_b, 6)}

    def z_first(kind, j):
        buf, fwd, own, _, _, base = bufs[kind]
        q = (base + j) * 4
        for k, dz in ((0, 1), (1, 3)):
            cp = remote(
                halves(buf.at[j, (z + 2) % 4], kind, k), fwd.at[j, k], zs.at[q + k], zr.at[q + k], dev(dz=dz)
            )
            cp.start()
            sent3.append(cp)
        width = 2 * T if kind == "d" else T
        cp = pltpu.make_async_copy(buf.at[j, z], own.at[:, pl.ds(j * width, width)], zl.at[base + j])
        cp.start()
        units[kind, j] = cp

    def z_second(kind, j):
        buf, fwd, _, out_a, out_b, base = bufs[kind]
        q = (base + j) * 4
        width = 2 * T if kind == "d" else T
        for k, dz, out in ((0, 1, out_a), (1, 3, out_b)):
            ref = fwd.at[j, k]
            remote(ref, ref, zs.at[q + k], zr.at[q + k], dev(dz=dz)).wait_recv()
            to = (z + dz) % 4
            if kind == "d":
                cols = pl.ds(k * T, T)
                buf[j, to, :, cols] = (buf[j, to, :, cols].astype(f32) + fwd[j, k].astype(f32)).astype(bf16)
            else:
                rows = pl.ds(k * 144, 144)
                buf[j, to, rows] = (buf[j, to, rows].astype(f32) + fwd[j, k].astype(f32)).astype(bf16)
            cp = remote(
                buf.at[j, to], out.at[:, pl.ds(j * width, width)], zs.at[q + 2 + k], zr.at[q + 2 + k], dev(dz=dz)
            )
            cp.start()
            sent3.append(cp)

    def down_grad(j):
        def one(i, _):
            lhs = ht[pl.ds(pl.multiple_of(yl * 576, 64), 576), :]
            cols = pl.ds(pl.multiple_of((j * 2 + i) * T, 128), T)
            rhs = mgbuf[:, :, :, :, :, cols].reshape(1024, T)
            zd[j, :, :, tile(i)] = nn(lhs, rhs).astype(bf16).reshape(4, 144, T)
            return 0

        lax.fori_loop(0, 2, one, 0)

    def hidden_grad(j):
        def one(k, _):
            a, b = k // 2, k % 2
            grad = nt(mgbuf[a, b].reshape(256, D), wd[pl.ds(j * T, T), :])
            cols = pl.ds(j * T, T)
            act[a, b, :, cols] = (grad * act[a, b, :, cols].astype(f32)).astype(bf16)
            us[a, b, :, cols] = (grad * us[a, b, :, cols].astype(f32)).astype(bf16)
            return 0

        lax.fori_loop(0, 4, one, 0)

    def in_grad(buf, src, j):
        def one(i, _):
            rhs = src[:, :, :, pl.ds(j * T, T)].reshape(1024, T)
            lhs = ntr[pl.ds(pl.multiple_of(i * 288, 32), 288), :]
            buf[j, i] = nn(lhs, rhs).astype(bf16)
            return 0

        lax.fori_loop(0, 4, one, 0)

    for j in range(3):
        down_grad(j)
        z_first("d", j)
    for j in range(3):
        hidden_grad(j)
        in_grad(zg, us, j)
        z_first("g", j)
        z_second("d", j)
        in_grad(zu, act, j)
        z_first("u", j)
        if j >= 1:
            z_second("g", j - 1)
            z_second("u", j - 1)

    def normed_grad(half):
        def one(j, _):
            total = nt(us[yl, half], wg[tile(j), :]) + nt(act[yl, half], wu[tile(j), :])
            part[half, :, :, :, tile(j)] = total.astype(bf16).reshape(4, 2, B, T)
            return 0

        lax.fori_loop(0, 6, one, 0)

    normed_grad(1 - yh)
    pend = [core_send(1 - yh, 0, rs2s, rs2r)]
    z_second("g", 2)
    z_second("u", 2)
    normed_grad(yh)
    pend.append(core_send(yh, 1, rs2s, rs2r))
    core_add(1 - yh, 0, rs2s, rs2r)
    pend += x_send(1 - yh, 0, rs2s, rs2r)
    core_add(yh, 1, rs2s, rs2r)
    pend += x_send(yh, 1, rs2s, rs2r)
    pend.append(y_send(x_sum(1 - yh, 0, rs2s, rs2r), rs2s, rs2r))
    grad_in = y_sum(x_sum(yh, 1, rs2s, rs2r), rs2s, rs2r)
    tok_f = tok[...].astype(f32)
    recip_in = lax.rsqrt(jnp.mean(tok_f * tok_f, axis=-1, keepdims=True) + epsilon)
    scaled_in = tok_f * recip_in
    weighted = grad_in * gpre[...]
    back = recip_in * (weighted - scaled_in * jnp.mean(weighted * scaled_in, axis=-1, keepdims=True))
    tgrad[...] = (cot[...].astype(f32) + back).astype(bf16)
    gv[0:1, :] = jnp.sum(grad_in * scaled_in, axis=0, keepdims=True)

    cp = remote(gv, gc, gs.at[0], gr.at[0], dev(dc=1))
    cp.start()
    cp.wait()
    value = gv[...] + gc[...]
    for n, (slots, axis, at) in enumerate(((gx, "dx", x), (gy, "dy", y), (gz, "dz", z))):
        slots[at] = value
        cps = []
        for k in (1, 2, 3):
            i = 1 + n * 3 + k - 1
            cp = remote(slots.at[at], slots.at[at], gs.at[i], gr.at[i], dev(**{axis: k}))
            cp.start()
            cps.append(cp)
        for k in (1, 2, 3):
            i = 1 + n * 3 + k - 1
            ref = slots.at[(at + 4 - k) % 4]
            remote(ref, ref, gs.at[i], gr.at[i], dev(**{axis: k})).wait_recv()
        for cp in cps:
            cp.wait_send()
        value = (slots[0] + slots[1]) + (slots[2] + slots[3])
    gain_pre_out[...] = value[0:1, :]
    gain_post_out[...] = value[1:2, :]

    for kind in "dgu":
        _, _, own, out_a, out_b, base = bufs[kind]
        width = 2 * T if kind == "d" else T
        for j in range(3):
            q = (base + j) * 4
            for k, out in ((0, out_a), (1, out_b)):
                ref = out.at[:, pl.ds(j * width, width)]
                remote(ref, ref, zs.at[q + 2 + k], zr.at[q + 2 + k], dev(dz=1)).wait_recv()
            units[kind, j].wait()
    for cp in pend + sent2 + sent3:
        cp.wait_send()


def local(tokens, gain_pre, gain_post, gate_weight, up_weight, down_weight, cotangent):
    vm = pl.BlockSpec(memory_space=pltpu.VMEM)
    hbm = pl.BlockSpec(memory_space=pl.ANY)
    S = jax.ShapeDtypeStruct
    dma = pltpu.SemaphoreType.DMA
    outs = pl.pallas_call(
        kernel,
        out_shape=(
            [S((B, D), bf16), S((B, D), bf16), S((1, D), f32), S((1, D), f32)]
            + [S((144, D), bf16)] * 3
            + [S((288, F), bf16)] * 6
        ),
        in_specs=[vm] * 4 + [hbm] * 3,
        out_specs=[vm] * 4 + [hbm] * 9,
        scratch_shapes=[
            pltpu.VMEM((D, F), bf16),
            pltpu.VMEM((D, F), bf16),
            pltpu.VMEM((F, D), bf16),
            pltpu.VMEM((2, 2, 4, 2, B, D), bf16),
            pltpu.VMEM((2, 2, 4, 2, B, D), bf16),
            pltpu.VMEM((2, 2, 256, F), bf16),
            pltpu.VMEM((2, 2, 256, F), bf16),
            pltpu.VMEM((2, 256, F), bf16),
            pltpu.VMEM((F, 1024), bf16),
            pltpu.VMEM((F, 1024), bf16),
            pltpu.VMEM((2, 4, 2, B, D), bf16),
            pltpu.VMEM((2, 4, B, D), bf16),
            pltpu.VMEM((2, 3, B, D), bf16),
            pltpu.VMEM((B, D), bf16),
            pltpu.VMEM((B, D), bf16),
            pltpu.VMEM((3, 4, 144, 2 * T), bf16),
            pltpu.VMEM((3, 4, 288, T), bf16),
            pltpu.VMEM((3, 4, 288, T), bf16),
            pltpu.VMEM((3, 2, 144, T), bf16),
            pltpu.VMEM((3, 2, 144, T), bf16),
            pltpu.VMEM((3, 2, 144, T), bf16),
            pltpu.VMEM((8, D), f32),
            pltpu.VMEM((8, D), f32),
            pltpu.VMEM((4, 8, D), f32),
            pltpu.VMEM((4, 8, D), f32),
            pltpu.VMEM((4, 8, D), f32),
            dma((3,)),
            dma((32,)), dma((32,)), dma((32,)), dma((32,)),
            dma((9,)), dma((9,)), dma((9,)), dma((9,)),
            dma((36,)), dma((36,)), dma((9,)),
            dma((10,)), dma((10,)),
        ],
        compiler_params=pltpu.CompilerParams(
            collective_id=0, has_side_effects=True, vmem_limit_bytes=62 * 2**20
        ),
        cost_estimate=pl.CostEstimate(flops=33 * 10**9, bytes_accessed=30 * 10**6, transcendentals=0),
    )(
        tokens, cotangent, gain_pre.reshape(1, D), gain_post.reshape(1, D),
        gate_weight, up_weight, down_weight,
    )
    block_out, tokens_grad, pre, post, *rest = outs

    def total(three):
        return (three[0].astype(f32) + three[1].astype(f32)) + three[2].astype(f32)

    return (
        block_out, tokens_grad, pre.reshape(D), post.reshape(D),
        total(rest[3:6]), total(rest[6:9]), total(rest[0:3]),
    )


def solution(mesh):
    in_specs = (
        P(("dp", "tp"), None),
        P(),
        P(),
        P(None, "tp"),
        P(None, "tp"),
        P("tp", None),
        P(("dp", "tp"), None),
    )
    out_specs = (
        P(("dp", "tp"), None),
        P(("dp", "tp"), None),
        P(),
        P(),
        P("dp", "tp"),
        P("dp", "tp"),
        P(("tp", "dp"), None),
    )
    return jax.shard_map(local, mesh=mesh, in_specs=in_specs, out_specs=out_specs, check_vma=False)
```

time: 514 us -> 179 us (0.35)
  waiting for transfers between devices: 222 us -> 0 us
  blocking collectives: 197 us -> 0 us
  Pallas kernels: 0 us -> 166 us
  matrix products: 61.7 us -> 0 us
  between operations: 14.2 us -> 0.74 us
  other arithmetic: 16.3 us -> 7.24 us
    psum x1 -> x0, blocking collectives: 197 us -> none  [local(): lax.psum((pre_term, post_term), ('dp', 'tp'))]
    pallas_call x0 -> x1, Pallas kernels: none -> 166 us  [local(): pl.pallas_call(kernel, out_shape=[S((B, D), bf16), S((B, D), bf16), S((1,...]
    reduce_scatter x5 -> x0, waiting for transfers between devices: 117 us -> none  [the longest x1 68.8 us: local(): lax.psum_scatter(jnp.dot(hidden, down_weight, preferred_element_type=jnp....]
    all_gather x2 -> x0, waiting for transfers between devices: 105 us -> none  [the longest x1 54 us: local(): shard_piece = lax.all_gather(normed, 'tp', axis=0, tiled=True)]
    dot_general x9 -> x0, matrix products: 61.7 us -> none  [the longest x3 22.6 us: contract_cols(): lax.dot_general(left_side, right_side, (((1,), (1,)), ((), ())), preferre...]
    convert_element_type x6 -> x0, other arithmetic: 11.9 us -> none  [the longest x3 6.71 us: local(): gate_grad, up_grad, down_grad = (lax.psum_scatter(gate_local.astype(jnp.b...]
    add x0 -> x2, other arithmetic: none -> 5.99 us  [total(): return three[0].astype(f32) + three[1].astype(f32) + three[2].astype(f32)]
  transfers between devices with their start and end apart: 7 -> 0, of which waited for: 4 -> 0; matrix products, arithmetic and copies ran while one was open for 5% -> 0% of each run, Pallas kernels for 0% -> 0%
where the time goes in v1:
time: 179 us; the launch traced here: 178 us
  Pallas kernels  166 us (93%)
  other arithmetic  7.24 us (4%)
  local copies, waits for them, and re-layouts  3.98 us (2%)
    pallas_call x1, Pallas kernels, local(): pl.pallas_call(kernel, out_shape=[S((B, D), bf16), S((B, D), bf16), S((1,...  166 us
    add x2, other arithmetic, total(): return three[0].astype(f32) + three[1].astype(f32) + three[2].astype(f32)  5.99 us

profile of v1, /device:TPU:1, one launch (start us, length us, event | category | flops | bytes accessed | tf_op | source)
XLA Modules:
  0.0 177.5 jit_solution(11662085376984208569)
XLA Ops:
  0.6 1.3 reshape.26.gpre
  1.9 1.3 reshape.27.gpost
  3.3 165.6 %shard_map.126 = (bf16[32,2304]{1,0:T(8,128)(2,1)}, bf16[32,2304]{1,0:T(8,128)(2,1)}, f32[1,2304]{1,0:T(1,128)}, f32[1,2304]{1,0:T(1,128)}, bf16[144,2304]{1,0:T...) custom-call(bf16[32,2304]{1,0:T(8,128)(2,1)} %tok.1, ...), custom_call_target="tpu_custom_call" | custom-call | flops 32999999488 | bytes 30000000 | tf_op jit(solution)/shard_map/pallas_call | solution.py:430
  168.8 0.0 copy-start
  168.8 0.0 copy-start.1
  168.9 0.0 copy-start.2
  168.9 0.0 copy-start.3
  168.9 0.0 copy-start.4
  168.9 2.9 %convert_add_fusion = f32[144,2304]{1,0:T(8,128)} fusion(bf16[144,2304]{1,0:T(8,128)(2,1)} %get-tuple-element.32, bf16[144,2304]{1,0:T(8,128)(2,1)} %get-tuple-element.31, bf16[144,2304]{1,0:T(8,128)(2,1)} %get-tuple-element.30), kind=kLoop, calls=%fused_computation | loop fusion | flops 1658880 | bytes 3317760 | tf_op jit(solution)/shard_map/add | solution.py:483
  171.8 0.0 copy-done
  171.8 0.0 copy-done.1
  171.8 0.0 copy-done.2
  171.8 0.0 copy-done.3
  171.8 0.0 copy-done.4
  171.8 0.0 copy-start.8
  171.8 0.0 copy-start.7
  171.9 0.0 copy-start.6
  171.9 0.0 copy-start.5
  171.9 3.1 %convert_add_fusion.1 = (f32[288,1152]{1,0:T(8,128)}, f32[288,1152]{1,0:T(8,128)}) fusion(bf16[288,1152]{1,0:T(8,128)(2,1)} %get-tuple-element.29, bf16[288,1152]{1,0:T(8,128)(2,1)S(1)} %copy-done.4, bf16[288,1152]{1,0:T(8,128)(2,1)S(1)} %copy-done.3, bf16[288,1152]{1,0:T(8,128)(2,1)S(1)} %copy-done.2, bf16[288,1152]{1,0:T(8,128)(2,1)S(1)} %copy-done.1, ...), kind=kLoop, calls=%fused_computation.1 | loop fusion | flops 3317760 | bytes 6635520 | tf_op jit(solution)/shard_map/add | solution.py:483
  174.9 0.0 copy-done.8
  174.9 0.6 reduce
  175.6 0.0 copy-done.7
  175.6 0.6 reduce.1
  176.2 0.0 copy-done.6
  176.2 0.7 copy.16
  176.9 0.0 copy-done.5
  176.9 0.7 copy.17
Async XLA Ops:
  168.8 3.0 %copy-start = (bf16[288,1152]{1,0:T(8,128)(2,1)S(1)}, bf16[288,1152]{1,0:T(8,128)(2,1)}, u32[]{:S(2)}) copy-start(bf16[288,1152]{1,0:T(8,128)(2,1)} %get-tuple-element.24) | copy-start | bytes 1990660
  168.8 3.0 %copy-start.1 = (bf16[288,1152]{1,0:T(8,128)(2,1)S(1)}, bf16[288,1152]{1,0:T(8,128)(2,1)}, u32[]{:S(2)}) copy-start(bf16[288,1152]{1,0:T(8,128)(2,1)} %get-tuple-element.25) | copy-start | bytes 1990660
  168.9 3.0 %copy-start.2 = (bf16[288,1152]{1,0:T(8,128)(2,1)S(1)}, bf16[288,1152]{1,0:T(8,128)(2,1)}, u32[]{:S(2)}) copy-start(bf16[288,1152]{1,0:T(8,128)(2,1)} %get-tuple-element.26) | copy-start | bytes 1990660
  168.9 3.0 %copy-start.3 = (bf16[288,1152]{1,0:T(8,128)(2,1)S(1)}, bf16[288,1152]{1,0:T(8,128)(2,1)}, u32[]{:S(2)}) copy-start(bf16[288,1152]{1,0:T(8,128)(2,1)} %get-tuple-element.27) | copy-start | bytes 1990660
  168.9 3.0 %copy-start.4 = (bf16[288,1152]{1,0:T(8,128)(2,1)S(1)}, bf16[288,1152]{1,0:T(8,128)(2,1)}, u32[]{:S(2)}) copy-start(bf16[288,1152]{1,0:T(8,128)(2,1)} %get-tuple-element.28) | copy-start | bytes 1990660
  171.8 3.1 %copy-start.8 = (f32[1,2304]{1,0:T(1,128)S(1)}, f32[1,2304]{1,0:T(1,128)}, u32[]{:S(2)}) copy-start(f32[1,2304]{1,0:T(1,128)} %get-tuple-element.22) | copy-start | bytes 27652
  171.8 3.7 %copy-start.7 = (f32[1,2304]{1,0:T(1,128)S(1)}, f32[1,2304]{1,0:T(1,128)}, u32[]{:S(2)}) copy-start(f32[1,2304]{1,0:T(1,128)} %get-tuple-element.23) | copy-start | bytes 27652
  171.9 4.3 %copy-start.6 = (bf16[32,2304]{1,0:T(8,128)(2,1)S(1)}, bf16[32,2304]{1,0:T(8,128)(2,1)}, u32[]{:S(2)}) copy-start(bf16[32,2304]{1,0:T(8,128)(2,1)} %get-tuple-element.42) | copy-start | bytes 442372
  171.9 5.0 %copy-start.5 = (bf16[32,2304]{1,0:T(8,128)(2,1)S(1)}, bf16[32,2304]{1,0:T(8,128)(2,1)}, u32[]{:S(2)}) copy-start(bf16[32,2304]{1,0:T(8,128)(2,1)} %get-tuple-element.43) | copy-start | bytes 442372

commit v2 on v1

v2 whole, which is shorter than its diff:
```python
import jax
import jax.numpy as jnp
from jax import lax
from jax.experimental import pallas as pl
from jax.experimental.pallas import tpu as pltpu
from jax.sharding import PartitionSpec as P

epsilon = 1e-06
root_two_pi = 0.7978845608028654
MESH = pl.DeviceIdType.MESH
D = 2304
F = 1152
B = 32
T = 384
W = 384
f32 = jnp.float32
bf16 = jnp.bfloat16


def gelu_pair(values):
    tanh_arg = root_two_pi * (values + 0.044715 * values * values * values)
    hyper = jnp.tanh(tanh_arg)
    gelu_value = 0.5 * values * (1.0 + hyper)
    gelu_slope = 0.5 * (1.0 + hyper) + 0.5 * values * (1.0 - hyper * hyper) * root_two_pi * (
        1.0 + 3.0 * 0.044715 * values * values
    )
    return (gelu_value, gelu_slope)


def nt(a, b):
    return lax.dot_general(a, b, (((1,), (1,)), ((), ())), preferred_element_type=f32)


def nn(a, b):
    return jnp.dot(a, b, preferred_element_type=f32)


def tile(j, width=T):
    return pl.ds(pl.multiple_of(j * width, 128), width)


def kernel(
    tok, cot, gpre_in, gpost_in, wg_h, wu_h, wd_h,
    bout, tgrad, gain_out, d_own, d_a, g_own, g_a, g_b, u_own, u_a, u_b,
    wg, wu, wd, nbuf, mgbuf, mzbuf, act, us, hown, ht, hz, ntr, part, crecv, xrecv, ysend, yrecv,
    zd, zg, zu, zgf, zuf, gate0, up0, gate1, up1, g_x, g_yz,
    wsem, ag1s, ag1r, ag2s, ag2r, ag3s, ag3r, rs1s, rs1r, rs2s, rs2r, zs, zr, zl, hs, hr, ms, mr, ds, dr, gs, gr,
):
    dp, tp = lax.axis_index("dp"), lax.axis_index("tp")
    c = tp % 2
    x = (tp // 2) % 4
    yh = tp // 8
    yl = dp // 4
    z = dp % 4
    y = yh * 2 + yl

    def dev(dx=0, dy=0, dz=0, dc=0):
        yy = (y + dy) % 4
        return ((yy % 2) * 4 + (z + dz) % 4, ((yy // 2) * 4 + (x + dx) % 4) * 2 + (c + dc) % 2)

    gate_up = ((gate0, up0), (gate1, up1))
    gpre = gpre_in[...].reshape(1, D)
    gpost = gpost_in[...].reshape(1, D)

    loads = [
        pltpu.make_async_copy(h, v, wsem.at[i])
        for i, (h, v) in enumerate(((wg_h, wg), (wu_h, wu), (wd_h, wd)))
    ]
    for load in loads:
        load.start()

    barrier = pltpu.get_barrier_semaphore()
    chips_x = [dict(dx=i, dc=j) for i in range(4) for j in range(2) if i + j]
    chips_yz = [dict(dy=i, dz=j) for i in range(4) for j in range(4) if i + j]
    offs = chips_x + chips_yz
    for o in offs:
        pl.semaphore_signal(barrier, inc=1, device_id=dev(**o), device_id_type=MESH)

    def remote(src, dst, s, r, to):
        return pltpu.make_async_remote_copy(
            src_ref=src, dst_ref=dst, send_sem=s, recv_sem=r, device_id=to, device_id_type=MESH
        )

    def blk(buf, df, ds, core=None):
        dx = df * (1 - c) + ds * c
        dy = df * c + ds * (1 - c)
        xx, yy = (x + dx) % 4, (y + dy) % 4
        return buf.at[yy % 2, yy // 2, xx, c]

    def other_blk(buf, df, ds):
        dx = df * c + ds * (1 - c)
        dy = df * (1 - c) + ds * c
        xx, yy = (x + dx) % 4, (y + dy) % 4
        return buf.at[yy % 2, yy // 2, xx, 1 - c]

    def to_f(sign):
        return dev(dx=(1 - c) * (sign % 4), dy=c * (sign % 4))

    def to_s(sign):
        return dev(dx=c * (sign % 4), dy=(1 - c) * (sign % 4))

    def gather(buf, ss, rr, sent):
        def send(i, ref, to):
            cp = remote(ref, ref, ss.at[i], rr.at[i], to)
            cp.start()
            sent.append(cp)

        def got(i, ref):
            remote(ref, ref, ss.at[i], rr.at[i], dev(dc=1)).wait_recv()

        def core(df, ds):
            send(16 + ds * 4 + df, blk(buf, df, ds), dev(dc=1))

        own = blk(buf, 0, 0)
        send(0, own, to_f(1))
        send(1, own, to_f(-1))
        send(4, own, to_s(1))
        send(8, own, to_s(-1))
        core(0, 0)
        yield
        got(0, blk(buf, 3, 0))
        send(2, blk(buf, 3, 0).at[pl.ds(0, 16)], to_f(1))
        send(7, blk(buf, 3, 0), to_s(1))
        send(11, blk(buf, 3, 0), to_s(-1))
        core(3, 0)
        got(1, blk(buf, 1, 0))
        send(3, blk(buf, 1, 0).at[pl.ds(16, 16)], to_f(-1))
        send(5, blk(buf, 1, 0), to_s(1))
        send(9, blk(buf, 1, 0), to_s(-1))
        core(1, 0)
        yield
        got(2, blk(buf, 2, 0).at[pl.ds(0, 16)])
        got(3, blk(buf, 2, 0).at[pl.ds(16, 16)])
        send(6, blk(buf, 2, 0), to_s(1))
        send(10, blk(buf, 2, 0), to_s(-1))
        core(2, 0)
        yield
        for df, fwd_a, fwd_b in ((0, 12, None), (1, 13, None), (3, None, 14), (2, None, 15)):
            got(4 + df, blk(buf, df, 3))
            if fwd_a is not None:
                send(fwd_a, blk(buf, df, 3), to_s(1))
            core(df, 3)
            got(8 + df, blk(buf, df, 1))
            if fwd_b is not None:
                send(fwd_b, blk(buf, df, 1), to_s(-1))
            core(df, 1)
            yield
        for i, df in ((12, 0), (13, 1), (14, 3), (15, 2)):
            got(i, blk(buf, df, 2))
            core(df, 2)
        yield
        for ds in range(4):
            for df in range(4):
                got(16 + ds * 4 + df, other_blk(buf, df, ds))

    def group_gather(buf, ss, rr, sent):
        def at(dx, dy, core=c):
            yy = (y + dy) % 4
            return buf.at[yy % 2, yy // 2, (x + dx) % 4, core]

        def send(i, ref, **to):
            cp = remote(ref, ref, ss.at[i], rr.at[i], dev(**to))
            cp.start()
            sent.append(cp)

        def got(i, ref):
            remote(ref, ref, ss.at[i], rr.at[i], dev(dc=1)).wait_recv()

        low, high = pl.ds(0, 16), pl.ds(16, 16)
        own = at(0, 0)
        send(0, own, dy=2)
        send(1, own, dx=1)
        send(2, own, dx=3)
        send(5, own, dc=1)
        send(3, own, dy=1)
        send(4, own, dy=3)
        got(0, at(0, 2))
        send(6, at(0, 2), dx=1)
        send(7, at(0, 2), dx=3)
        send(8, at(0, 2), dc=1)
        got(1, at(3, 0))
        send(9, at(3, 0).at[low], dx=1)
        send(12, at(3, 0), dc=1)
        got(2, at(1, 0))
        send(13, at(1, 0).at[high], dx=3)
        send(16, at(1, 0), dc=1)
        for i, dx in ((10, 3), (14, 1)):
            send(i, at(dx, 0), dy=1)
            send(i + 1, at(dx, 0), dy=3)
        got(6, at(3, 2))
        send(20, at(3, 2).at[low], dx=1)
        send(21, at(3, 2), dc=1)
        got(7, at(1, 2))
        send(22, at(1, 2).at[high], dx=3)
        send(23, at(1, 2), dc=1)
        got(9, at(2, 0).at[low])
        got(13, at(2, 0).at[high])
        send(19, at(2, 0), dc=1)
        send(17, at(2, 0), dy=1)
        send(18, at(2, 0), dy=3)
        got(20, at(2, 2).at[low])
        got(22, at(2, 2).at[high])
        send(24, at(2, 2), dc=1)
        for i, dx, dy in ((5, 0, 0), (8, 0, 2), (12, 3, 0), (16, 1, 0), (21, 3, 2), (23, 1, 2), (19, 2, 0), (24, 2, 2)):
            got(i, at(dx, dy, 1 - c))
        yield
        rest = [(i + k, dx, 3 - 2 * k) for i, dx in ((3, 0), (10, 3), (14, 1), (17, 2)) for k in (0, 1)]
        for n, (i, dx, dy) in enumerate(rest):
            got(i, at(dx, dy))
            send(25 + n, at(dx, dy), dc=1)
        yield
        for n, (i, dx, dy) in enumerate(rest):
            got(25 + n, at(dx, dy, 1 - c))

    def run(steps):
        for _ in steps:
            pass

    def core_send(half, i, ss, rr):
        cp = remote(part.at[half, :, 1 - c], crecv.at[i], ss.at[i], rr.at[i], dev(dc=1))
        cp.start()
        return cp

    def core_add(half, i, ss, rr):
        remote(crecv.at[i], crecv.at[i], ss.at[i], rr.at[i], dev(dc=1)).wait_recv()

        def one(k, _):
            part[half, k, c] = (part[half, k, c].astype(f32) + crecv[i, k].astype(f32)).astype(bf16)
            return 0

        lax.fori_loop(0, 4, one, 0)

    def x_send(half, i, ss, rr):
        out = []
        for dx in (2, 1, 3):
            k = 2 + i * 3 + dx - 1
            cp = remote(
                part.at[half, (x + dx) % 4, c], xrecv.at[i, dx - 1], ss.at[k], rr.at[k], dev(dx=dx)
            )
            cp.start()
            out.append(cp)
        return out

    def x_sum(half, i, ss, rr):
        for dx in (1, 3, 2):
            k = 2 + i * 3 + dx - 1
            ref = xrecv.at[i, dx - 1]
            remote(ref, ref, ss.at[k], rr.at[k], dev(dx=dx)).wait_recv()
        total = part[half, x, c].astype(f32)
        for dx in (1, 3, 2):
            total = total + xrecv[i, dx - 1].astype(f32)
        return total

    def y_send(total, ss, rr):
        ysend[...] = total.astype(bf16)
        cp = remote(ysend, yrecv, ss.at[8], rr.at[8], dev(dy=2))
        cp.start()
        return cp

    def y_sum(total, ss, rr):
        remote(yrecv, yrecv, ss.at[8], rr.at[8], dev(dy=2)).wait_recv()
        return total + yrecv[...].astype(f32)

    tok_f = tok[...].astype(f32)
    recip_in = lax.rsqrt(jnp.mean(tok_f * tok_f, axis=-1, keepdims=True) + epsilon)
    nbuf[yl, yh, x, c] = (tok_f * recip_in * gpre).astype(bf16)

    pl.semaphore_wait(barrier, len(offs))
    sent1 = []
    steps = group_gather(nbuf, ag1s, ag1r, sent1)
    next(steps)
    for load in loads:
        load.wait()

    def forward(a, b, is_own):
        rows = nbuf[a, b].reshape(256, D)
        for j in range(4):
            if j < 3:
                gate_up[j % 2][0][...] = nn(rows, wg[:, pl.ds(j * T, T)])
                gate_up[j % 2][1][...] = nn(rows, wu[:, pl.ds(j * T, T)])
            if j > 0:
                cols = pl.ds((j - 1) * T, T)
                up = gate_up[(j - 1) % 2][1][...]
                value, slope = gelu_pair(gate_up[(j - 1) % 2][0][...])
                hidden = (value * up).astype(bf16)
                act[a, b, :, cols] = value.astype(bf16)
                us[a, b, :, cols] = (up * slope).astype(bf16)
                if is_own:
                    hown[b, :, cols] = hidden
                ht[cols, tile(a * 2 + b, 256)] = hidden.T

    def down(half):
        def one(j, _):
            part[half, :, :, :, tile(j)] = (
                nn(hown[half], wd[:, tile(j)]).astype(bf16).reshape(4, 2, B, T)
            )
            return 0

        lax.fori_loop(0, 6, one, 0)

    forward(yl, 1 - yh, True)
    down(1 - yh)
    pend = [core_send(1 - yh, 0, rs1s, rs1r)]
    forward(yl, yh, True)
    core_add(1 - yh, 0, rs1s, rs1r)
    pend += x_send(1 - yh, 0, rs1s, rs1r)
    down(yh)
    pend.append(core_send(yh, 1, rs1s, rs1r))
    next(steps)
    core_add(yh, 1, rs1s, rs1r)
    pend += x_send(yh, 1, rs1s, rs1r)
    run(steps)
    forward(1 - yl, 0, False)
    pend.append(y_send(x_sum(1 - yh, 0, rs1s, rs1r), rs1s, rs1r))
    forward(1 - yl, 1, False)

    sent2 = []
    near = (z + 1 - 2 * (z % 2), 3 - z)
    step = (1 + 2 * (z % 2), 3 - 2 * (z % 2))

    def shards(q):
        flip = q + 1 - 2 * (q % 2)
        return ((q, 3 - q), (q, flip))

    def ht_rows(q):
        return pl.ds(pl.multiple_of((yl * 4 + q) * 144, 16), 144)

    for h in range(2):
        for i in range(2):
            cp = remote(ht.at[ht_rows(shards(near[h])[h][i])], hz.at[h, i], hs.at[h * 2 + i], hr.at[h * 2 + i], dev(dz=step[h]))
            cp.start()
            sent2.append(cp)

    mixed = y_sum(x_sum(yh, 1, rs1s, rs1r), rs1s, rs1r)

    recip_mix = lax.rsqrt(jnp.mean(mixed * mixed, axis=-1, keepdims=True) + epsilon)
    scaled_mix = mixed * recip_mix
    cot_f = cot[...].astype(f32)
    weighted = cot_f * gpost
    mix_grad = recip_mix * (
        weighted - scaled_mix * jnp.mean(weighted * scaled_mix, axis=-1, keepdims=True)
    )
    mgbuf[yl, yh, x, c] = mix_grad.astype(bf16)
    bout[...] = (tok[...].astype(f32) + scaled_mix * gpost).astype(bf16)
    g_x[x * 2 + c, 1:2, :] = jnp.sum(cot_f * scaled_mix, axis=0, keepdims=True)
    for cp in pend + sent1:
        cp.wait_send()

    def mz_half(h):
        return (pl.ds(0, B), pl.ds(h * F, F))

    for h in range(2):
        cp = remote(
            mgbuf.at[yl, yh, x, c].at[mz_half(h)], mzbuf.at[yl, yh, x, c].at[mz_half(h)], ms.at[h], mr.at[h], dev(dz=step[h])
        )
        cp.start()
        sent2.append(cp)
    run(gather(mgbuf, ag2s, ag2r, sent2))

    def turn(k, _):
        def one(j, _):
            cols = pl.ds(pl.multiple_of(yl * F + j * T, 128), T)
            ntr[tile(j), tile(k, 256)] = nbuf[k // 2, k % 2, :, :, :, cols].reshape(256, T).T
            return 0

        lax.fori_loop(0, 3, one, 0)
        return 0

    lax.fori_loop(0, 4, turn, 0)

    units = {}
    sent3 = []

    bufs = {"g": (zg, zgf, g_own, g_a, g_b, 0), "u": (zu, zuf, u_own, u_a, u_b, 3)}

    def z_first(kind, j):
        buf, fwd, own, _, _, base = bufs[kind]
        q = (base + j) * 4
        for k, dz in ((0, 1), (1, 3)):
            cp = remote(
                buf.at[j, (z + 2) % 4].at[pl.ds(k * 144, 144)], fwd.at[j, k], zs.at[q + k], zr.at[q + k], dev(dz=dz)
            )
            cp.start()
            sent3.append(cp)
        cp = pltpu.make_async_copy(buf.at[j, z], own.at[:, pl.ds(j * T, T)], zl.at[base + j])
        cp.start()
        units[kind, j] = cp

    def z_second(kind, j):
        buf, fwd, _, out_a, out_b, base = bufs[kind]
        q = (base + j) * 4
        for k, dz, out in ((0, 1, out_a), (1, 3, out_b)):
            ref = fwd.at[j, k]
            remote(ref, ref, zs.at[q + k], zr.at[q + k], dev(dz=dz)).wait_recv()
            to = (z + dz) % 4
            rows = pl.ds(k * 144, 144)
            buf[j, to, rows] = (buf[j, to, rows].astype(f32) + fwd[j, k].astype(f32)).astype(bf16)
            cp = remote(
                buf.at[j, to], out.at[:, pl.ds(j * T, T)], zs.at[q + 2 + k], zr.at[q + 2 + k], dev(dz=dz)
            )
            cp.start()
            sent3.append(cp)

    def down_grad(h):
        for i in range(2):
            ref = hz.at[h, i]
            remote(ref, ref, hs.at[h * 2 + i], hr.at[h * 2 + i], dev(dz=step[h])).wait_recv()
        mine = shards(z)[h]
        for i in range(2):

            def one(j, _, i=i):
                cols = pl.ds(pl.multiple_of(h * F + j * T, 128), T)
                total = nn(ht[ht_rows(mine[i]), :], mgbuf[:, :, :, :, :, cols].reshape(1024, T))
                total = total + nn(hz[h, i], mzbuf[:, :, :, :, :, cols].reshape(1024, T))
                zd[h, i, :, tile(j)] = total.astype(bf16)
                return 0

            lax.fori_loop(0, 3, one, 0)
        cp = remote(zd.at[h, 1], d_a.at[:, pl.ds(h * F, F)], ds.at[h], dr.at[h], dev(dz=step[1 - h]))
        cp.start()
        sent3.append(cp)
        cp = pltpu.make_async_copy(zd.at[h, 0], d_own.at[:, pl.ds(h * F, F)], zl.at[6 + h])
        cp.start()
        units["d", h] = cp

    def hidden_grad(j):
        def one(k, _):
            a, b = k // 2, k % 2
            grad = nt(mgbuf[a, b].reshape(256, D), wd[pl.ds(j * T, T), :])
            cols = pl.ds(j * T, T)
            act[a, b, :, cols] = (grad * act[a, b, :, cols].astype(f32)).astype(bf16)
            us[a, b, :, cols] = (grad * us[a, b, :, cols].astype(f32)).astype(bf16)
            return 0

        lax.fori_loop(0, 4, one, 0)

    def in_grad(buf, src, j):
        def one(i, _):
            rhs = src[:, :, :, pl.ds(j * T, T)].reshape(1024, T)
            lhs = ntr[pl.ds(pl.multiple_of(i * 288, 32), 288), :]
            buf[j, i] = nn(lhs, rhs).astype(bf16)
            return 0

        lax.fori_loop(0, 4, one, 0)

    for h in range(2):
        ref = mzbuf.at[yl, yh, x, c].at[mz_half(h)]
        remote(ref, ref, ms.at[h], mr.at[h], dev(dz=step[h])).wait_recv()
    steps = gather(mzbuf, ag3s, ag3r, sent2)
    next(steps)
    for j in range(3):
        hidden_grad(j)
        next(steps, None)
        in_grad(zg, us, j)
        z_first("g", j)
        next(steps, None)
        if j >= 1:
            z_second("g", j - 1)
        in_grad(zu, act, j)
        z_first("u", j)
        next(steps, None)
        if j >= 1:
            z_second("u", j - 1)

    def normed_grad(half):
        def one(j, _):
            total = nt(us[yl, half], wg[tile(j), :]) + nt(act[yl, half], wu[tile(j), :])
            part[half, :, :, :, tile(j)] = total.astype(bf16).reshape(4, 2, B, T)
            return 0

        lax.fori_loop(0, 6, one, 0)

    normed_grad(1 - yh)
    pend = [core_send(1 - yh, 0, rs2s, rs2r)]
    next(steps, None)
    normed_grad(yh)
    pend.append(core_send(yh, 1, rs2s, rs2r))
    core_add(1 - yh, 0, rs2s, rs2r)
    pend += x_send(1 - yh, 0, rs2s, rs2r)
    next(steps, None)
    core_add(yh, 1, rs2s, rs2r)
    pend += x_send(yh, 1, rs2s, rs2r)
    z_second("g", 2)
    run(steps)
    down_grad(0)
    pend.append(y_send(x_sum(1 - yh, 0, rs2s, rs2r), rs2s, rs2r))
    z_second("u", 2)
    down_grad(1)
    grad_in = y_sum(x_sum(yh, 1, rs2s, rs2r), rs2s, rs2r)
    tok_f = tok[...].astype(f32)
    recip_in = lax.rsqrt(jnp.mean(tok_f * tok_f, axis=-1, keepdims=True) + epsilon)
    scaled_in = tok_f * recip_in
    weighted = grad_in * gpre
    back = recip_in * (weighted - scaled_in * jnp.mean(weighted * scaled_in, axis=-1, keepdims=True))
    tgrad[...] = (cot[...].astype(f32) + back).astype(bf16)
    g_x[x * 2 + c, 0:1, :] = jnp.sum(grad_in * scaled_in, axis=0, keepdims=True)

    def exchange(slots, me, peers, base, place):
        cps = []
        for n, o in enumerate(peers):
            cp = remote(slots.at[me], slots.at[me], gs.at[base + n], gr.at[base + n], dev(**o))
            cp.start()
            cps.append(cp)
        for n, o in enumerate(peers):
            ref = slots.at[place({k: -v for k, v in o.items()})]
            remote(ref, ref, gs.at[base + n], gr.at[base + n], dev(**o)).wait_recv()
        value = slots[0]
        for n in range(1, len(peers) + 1):
            value = value + slots[n]
        return value, cps

    value, cps = exchange(
        g_x, x * 2 + c, chips_x, 0, lambda o: ((x + o["dx"] + 4) % 4) * 2 + (c + o["dc"] + 2) % 2
    )
    sent3 += cps
    g_yz[y * 4 + z] = value
    value, cps = exchange(
        g_yz, y * 4 + z, chips_yz, 7, lambda o: ((y + o["dy"] + 4) % 4) * 4 + (z + o["dz"] + 4) % 4
    )
    sent3 += cps
    gain_out[...] = value

    for kind in "gu":
        _, _, own, out_a, out_b, base = bufs[kind]
        for j in range(3):
            q = (base + j) * 4
            for k, out in ((0, out_a), (1, out_b)):
                ref = out.at[:, pl.ds(j * T, T)]
                remote(ref, ref, zs.at[q + 2 + k], zr.at[q + 2 + k], dev(dz=1)).wait_recv()
            units[kind, j].wait()
    for h in range(2):
        ref = d_a.at[:, pl.ds(h * F, F)]
        remote(ref, ref, ds.at[h], dr.at[h], dev(dz=1)).wait_recv()
        units["d", h].wait()
    for cp in pend + sent2 + sent3:
        cp.wait_send()


def finish(
    bout, tgrad, gains, d_own, d_a, g_own, g_a, g_b, u_own, u_a, u_b,
    bout_out, tgrad_out, pre_out, post_out, gate_out, up_out, down_out,
):
    bout_out[...] = bout[...]
    tgrad_out[...] = tgrad[...]
    pre_out[...] = gains[0, :]
    post_out[...] = gains[1, :]
    gate_out[...] = (g_own[...].astype(f32) + g_a[...].astype(f32)) + g_b[...].astype(f32)
    up_out[...] = (u_own[...].astype(f32) + u_a[...].astype(f32)) + u_b[...].astype(f32)
    down_out[...] = d_own[...].astype(f32) + d_a[...].astype(f32)


def local(tokens, gain_pre, gain_post, gate_weight, up_weight, down_weight, cotangent):
    vm = pl.BlockSpec(memory_space=pltpu.VMEM)
    hbm = pl.BlockSpec(memory_space=pl.ANY)
    S = jax.ShapeDtypeStruct
    dma = pltpu.SemaphoreType.DMA
    V = pltpu.VMEM
    outs = pl.pallas_call(
        kernel,
        out_shape=(
            [S((B, D), bf16), S((B, D), bf16), S((2, D), f32)]
            + [S((144, D), bf16)] * 2
            + [S((288, F), bf16)] * 6
        ),
        in_specs=[vm] * 4 + [hbm] * 3,
        out_specs=[vm] * 3 + [hbm] * 8,
        scratch_shapes=[
            V((D, F), bf16),
            V((D, F), bf16),
            V((F, D), bf16),
            V((2, 2, 4, 2, B, D), bf16),
            V((2, 2, 4, 2, B, D), bf16),
            V((2, 2, 4, 2, B, D), bf16),
            V((2, 2, 256, F), bf16),
            V((2, 2, 256, F), bf16),
            V((2, 256, F), bf16),
            V((F, 1024), bf16),
            V((2, 2, 144, 1024), bf16),
            V((F, 1024), bf16),
            V((2, 4, 2, B, D), bf16),
            V((2, 4, B, D), bf16),
            V((2, 3, B, D), bf16),
            V((B, D), bf16),
            V((B, D), bf16),
            V((2, 2, 144, F), bf16),
            V((3, 4, 288, T), bf16),
            V((3, 4, 288, T), bf16),
            V((3, 2, 144, T), bf16),
            V((3, 2, 144, T), bf16),
            V((256, T), f32),
            V((256, T), f32),
            V((256, T), f32),
            V((256, T), f32),
            V((8, 2, D), f32),
            V((16, 2, D), f32),
            dma((3,)),
            dma((33,)), dma((33,)), dma((32,)), dma((32,)), dma((32,)), dma((32,)),
            dma((9,)), dma((9,)), dma((9,)), dma((9,)),
            dma((24,)), dma((24,)), dma((8,)),
            dma((4,)), dma((4,)), dma((2,)), dma((2,)), dma((2,)), dma((2,)),
            dma((22,)), dma((22,)),
        ],
        compiler_params=pltpu.CompilerParams(
            collective_id=0, has_side_effects=True, vmem_limit_bytes=63 * 2**20
        ),
        cost_estimate=pl.CostEstimate(flops=33 * 10**9, bytes_accessed=30 * 10**6, transcendentals=0),
    )(
        tokens, cotangent, gain_pre, gain_post,
        gate_weight, up_weight, down_weight,
    )

    def whole(*shape):
        return pl.BlockSpec(shape, lambda i: (0,) * len(shape))

    def rows(n, width):
        return pl.BlockSpec((n, width), lambda i: (i, 0))

    n = 3
    return pl.pallas_call(
        finish,
        grid=(n,),
        out_shape=[
            S((B, D), bf16), S((B, D), bf16), S((D,), f32), S((D,), f32),
            S((288, F), f32), S((288, F), f32), S((144, D), f32),
        ],
        in_specs=[whole(B, D), whole(B, D), whole(2, D)] + [rows(144 // n, D)] * 2 + [rows(288 // n, F)] * 6,
        out_specs=[whole(B, D), whole(B, D), whole(D), whole(D)]
        + [rows(288 // n, F)] * 2 + [rows(144 // n, D)],
    )(*outs)


def solution(mesh):
    in_specs = (
        P(("dp", "tp"), None),
        P(),
        P(),
        P(None, "tp"),
        P(None, "tp"),
        P("tp", None),
        P(("dp", "tp"), None),
    )
    out_specs = (
        P(("dp", "tp"), None),
        P(("dp", "tp"), None),
        P(),
        P(),
        P("dp", "tp"),
        P("dp", "tp"),
        P(("tp", "dp"), None),
    )
    return jax.shard_map(local, mesh=mesh, in_specs=in_specs, out_specs=out_specs, check_vma=False)
```

time: 179 us -> 150 us (0.84)
  Pallas kernels: 166 us -> 148 us
  other arithmetic: 7.24 us -> 0 us
  local copies, waits for them, and re-layouts: 3.98 us -> 0 us
    pallas_call x1 -> x2, Pallas kernels: 166 us -> 148 us  [the longest x1 143 us: local(): pl.pallas_call(kernel, out_shape=[S((B, D), bf16), S((B, D), bf16), S((2,...]
    add x2 -> x0, other arithmetic: 5.99 us -> none  [total(): return three[0].astype(f32) + three[1].astype(f32) + three[2].astype(f32)]
    reshape x2 -> x0, local copies, waits for them, and re-layouts: 2.62 us -> none  [the longest x1 1.31 us: local(): gain_pre.reshape(1, D)]
where the time goes in v2:
time: 150 us; the launch traced here: 149 us
  Pallas kernels  148 us (99%)
    pallas_call x1, Pallas kernels, local(): pl.pallas_call(kernel, out_shape=[S((B, D), bf16), S((B, D), bf16), S((2,...  143 us
    pallas_call x1, Pallas kernels, local(): pl.pallas_call(finish, grid=(n,), out_shape=[S((B, D), bf16), S((B, D), b...  5.76 us

profile of v2, /device:TPU:1, one launch (start us, length us, event | category | flops | bytes accessed | tf_op | source)
XLA Modules:
  0.0 149.2 jit_solution(15777300650914900068)
XLA Ops:
  0.6 142.6 %shard_map.126 = (bf16[32,2304]{1,0:T(8,128)(2,1)}, bf16[32,2304]{1,0:T(8,128)(2,1)}, f32[2,2304]{1,0:T(2,128)}, bf16[144,2304]{1,0:T(8,128)(2,1)}, bf16[144,230...) custom-call(bf16[32,2304]{1,0:T(8,128)(2,1)} %tok.1, ...), custom_call_target="tpu_custom_call" | custom-call | flops 32999999488 | bytes 30000000 | tf_op jit(solution)/shard_map/pallas_call | solution.py:558
  143.2 5.8 %shard_map.127 = (bf16[32,2304]{1,0:T(8,128)(2,1)}, bf16[32,2304]{1,0:T(8,128)(2,1)}, f32[2304]{0:T(1024)}, f32[2304]{0:T(1024)}, f32[288,1152]{1,0:T(8,128)}, /*index=5*/f32[288,1152]{1,0:T(8,128)}, f32[144,2304]{1,0:T(8,128)}) custom-call(bf16[32,2304]{1,0:T(8,128)(2,1)} %get-tuple-element.18.bout, bf16[32,2304]{1,0:T(8,128)(2,1)} %get-tuple-element.19.tgrad, ...), custom_call_target="tpu_custom_call" | custom-call | tf_op jit(solution)/shard_map/pallas_call | solution.py:619

commit v3 on v2

--- a/solution.py
+++ b/solution.py
@@ -12,7 +12,6 @@
 F = 1152
 B = 32
 T = 384
-W = 384
 f32 = jnp.float32
 bf16 = jnp.bfloat16
 
@@ -42,8 +41,8 @@
 def kernel(
     tok, cot, gpre_in, gpost_in, wg_h, wu_h, wd_h,
     bout, tgrad, gain_out, d_own, d_a, g_own, g_a, g_b, u_own, u_a, u_b,
-    wg, wu, wd, nbuf, mgbuf, mzbuf, act, us, hown, ht, hz, ntr, part, crecv, xrecv, ysend, yrecv,
-    zd, zg, zu, zgf, zuf, gate0, up0, gate1, up1, g_x, g_yz,
+    wgu, wd, nbuf, mgbuf, mzbuf, au, hown, ht, hz, ntr, part, crecv, xrecv, ysend, yrecv, yall,
+    zd, zg, zu, zgf, zuf, gu0, gu1, g_x, g_yz,
     wsem, ag1s, ag1r, ag2s, ag2r, ag3s, ag3r, rs1s, rs1r, rs2s, rs2r, zs, zr, zl, hs, hr, ms, mr, ds, dr, gs, gr,
 ):
     dp, tp = lax.axis_index("dp"), lax.axis_index("tp")
@@ -58,16 +57,17 @@
         yy = (y + dy) % 4
         return ((yy % 2) * 4 + (z + dz) % 4, ((yy // 2) * 4 + (x + dx) % 4) * 2 + (c + dc) % 2)
 
-    gate_up = ((gate0, up0), (gate1, up1))
+    gate_up = (gu0, gu1)
     gpre = gpre_in[...].reshape(1, D)
     gpost = gpost_in[...].reshape(1, D)
 
     loads = [
-        pltpu.make_async_copy(h, v, wsem.at[i])
-        for i, (h, v) in enumerate(((wg_h, wg), (wu_h, wu), (wd_h, wd)))
-    ]
-    for load in loads:
-        load.start()
+        pltpu.make_async_copy(
+            h.at[:, pl.ds(j * T, T)], wgu.at[:, pl.ds((2 * j + k) * T, T)], wsem.at[2 * j + k]
+        )
+        for j in range(3)
+        for k, h in enumerate((wg_h, wu_h))
+    ] + [pltpu.make_async_copy(wd_h, wd, wsem.at[6])]
 
     barrier = pltpu.get_barrier_semaphore()
     chips_x = [dict(dx=i, dc=j) for i in range(4) for j in range(2) if i + j]
@@ -172,12 +172,14 @@
         send(1, own, dx=1)
         send(2, own, dx=3)
         send(5, own, dc=1)
-        send(3, own, dy=1)
-        send(4, own, dy=3)
+        yield
         got(0, at(0, 2))
         send(6, at(0, 2), dx=1)
         send(7, at(0, 2), dx=3)
         send(8, at(0, 2), dc=1)
+        send(3, own, dy=1)
+        send(4, own, dy=3)
+        yield
         got(1, at(3, 0))
         send(9, at(3, 0).at[low], dx=1)
         send(12, at(3, 0), dc=1)
@@ -187,6 +189,7 @@
         for i, dx in ((10, 3), (14, 1)):
             send(i, at(dx, 0), dy=1)
             send(i + 1, at(dx, 0), dy=3)
+        yield
         got(6, at(3, 2))
         send(20, at(3, 2).at[low], dx=1)
         send(21, at(3, 2), dc=1)
@@ -230,15 +233,13 @@
 
         lax.fori_loop(0, 4, one, 0)
 
-    def x_send(half, i, ss, rr):
+    def x_copies(half, i, ss, rr):
         out = []
         for dx in (2, 1, 3):
             k = 2 + i * 3 + dx - 1
-            cp = remote(
+            out.append(remote(
                 part.at[half, (x + dx) % 4, c], xrecv.at[i, dx - 1], ss.at[k], rr.at[k], dev(dx=dx)
-            )
-            cp.start()
-            out.append(cp)
+            ))
         return out
 
     def x_sum(half, i, ss, rr):
@@ -251,15 +252,76 @@
             total = total + xrecv[i, dx - 1].astype(f32)
         return total
 
-    def y_send(total, ss, rr):
-        ysend[...] = total.astype(bf16)
-        cp = remote(ysend, yrecv, ss.at[8], rr.at[8], dev(dy=2))
-        cp.start()
-        return cp
-
-    def y_sum(total, ss, rr):
-        remote(yrecv, yrecv, ss.at[8], rr.at[8], dev(dy=2)).wait_recv()
+    def y_copy(ss, rr):
+        return remote(ysend, yrecv, ss.at[8], rr.at[8], dev(dy=2))
+
+    def y_copy_all(ss, rr):
+        return remote(part.at[1 - yh, :, c], yall, ss.at[8], rr.at[8], dev(dy=2))
+
+    def start(copies):
+        for cp in copies:
+            cp.start()
+
+    def sum_first(ss, rr):
+        core_add(1 - yh, 0, ss, rr)
+
+        @pl.when(c == 0)
+        def _():
+            start(x_copies(1 - yh, 0, ss, rr))
+
+        @pl.when(c == 1)
+        def _():
+            start([y_copy_all(ss, rr)])
+
+    def sum_second(ss, rr):
+        core_add(yh, 1, ss, rr)
+
+        @pl.when(c == 0)
+        def _():
+            start(x_copies(yh, 1, ss, rr))
+
+    def sum_third(ss, rr):
+        @pl.when(c == 0)
+        def _():
+            ysend[...] = x_sum(1 - yh, 0, ss, rr).astype(bf16)
+            start([y_copy(ss, rr)])
+
+        @pl.when(c == 1)
+        def _():
+            y_copy_all(ss, rr).wait_recv()
+
+            def one(k, _):
+                part[yh, k, c] = (part[yh, k, c].astype(f32) + yall[k].astype(f32)).astype(bf16)
+                return 0
+
+            lax.fori_loop(0, 4, one, 0)
+            start(x_copies(yh, 1, ss, rr))
+
+    def sum_last(ss, rr):
+        total = x_sum(yh, 1, ss, rr)
+
+        @pl.when(c == 0)
+        def _():
+            y_copy(ss, rr).wait_recv()
+
         return total + yrecv[...].astype(f32)
+
+    def sum_wait(ss, rr):
+        @pl.when(c == 0)
+        def _():
+            for cp in x_copies(1 - yh, 0, ss, rr) + [y_copy(ss, rr)]:
+                cp.wait_send()
+
+        @pl.when(c == 1)
+        def _():
+            y_copy_all(ss, rr).wait_send()
+
+        for cp in x_copies(yh, 1, ss, rr):
+            cp.wait_send()
+
+    @pl.when(c == 1)
+    def _():
+        yrecv[...] = jnp.zeros_like(yrecv)
 
     tok_f = tok[...].astype(f32)
     recip_in = lax.rsqrt(jnp.mean(tok_f * tok_f, axis=-1, keepdims=True) + epsilon)
@@ -268,50 +330,53 @@
     pl.semaphore_wait(barrier, len(offs))
     sent1 = []
     steps = group_gather(nbuf, ag1s, ag1r, sent1)
+    for some in (loads[0:2], loads[2:4], loads[4:7]):
+        next(steps)
+        for load in some:
+            load.start()
     next(steps)
     for load in loads:
         load.wait()
 
-    def forward(a, b, is_own):
+    def forward(a, b, is_own, between=None):
         rows = nbuf[a, b].reshape(256, D)
         for j in range(4):
             if j < 3:
-                gate_up[j % 2][0][...] = nn(rows, wg[:, pl.ds(j * T, T)])
-                gate_up[j % 2][1][...] = nn(rows, wu[:, pl.ds(j * T, T)])
+                gate_up[j % 2][...] = nn(rows, wgu[:, pl.ds(j * 2 * T, 2 * T)])
             if j > 0:
                 cols = pl.ds((j - 1) * T, T)
-                up = gate_up[(j - 1) % 2][1][...]
-                value, slope = gelu_pair(gate_up[(j - 1) % 2][0][...])
+                up = gate_up[(j - 1) % 2][:, T:]
+                value, slope = gelu_pair(gate_up[(j - 1) % 2][:, :T])
                 hidden = (value * up).astype(bf16)
-                act[a, b, :, cols] = value.astype(bf16)
-                us[a, b, :, cols] = (up * slope).astype(bf16)
+                au[a, b, :, pl.ds((j - 1) * 2 * T, T)] = (up * slope).astype(bf16)
+                au[a, b, :, pl.ds((j - 1) * 2 * T + T, T)] = value.astype(bf16)
                 if is_own:
                     hown[b, :, cols] = hidden
                 ht[cols, tile(a * 2 + b, 256)] = hidden.T
+            if between is not None and j == 1:
+                between()
 
     def down(half):
         def one(j, _):
-            part[half, :, :, :, tile(j)] = (
-                nn(hown[half], wd[:, tile(j)]).astype(bf16).reshape(4, 2, B, T)
+            part[half, :, :, :, tile(j, 2 * T)] = (
+                nn(hown[half], wd[:, tile(j, 2 * T)]).astype(bf16).reshape(4, 2, B, 2 * T)
             )
             return 0
 
-        lax.fori_loop(0, 6, one, 0)
+        lax.fori_loop(0, 3, one, 0)
 
     forward(yl, 1 - yh, True)
     down(1 - yh)
     pend = [core_send(1 - yh, 0, rs1s, rs1r)]
-    forward(yl, yh, True)
-    core_add(1 - yh, 0, rs1s, rs1r)
-    pend += x_send(1 - yh, 0, rs1s, rs1r)
+
+    forward(yl, yh, True, lambda: sum_first(rs1s, rs1r))
     down(yh)
     pend.append(core_send(yh, 1, rs1s, rs1r))
     next(steps)
-    core_add(yh, 1, rs1s, rs1r)
-    pend += x_send(yh, 1, rs1s, rs1r)
+    sum_second(rs1s, rs1r)
     run(steps)
     forward(1 - yl, 0, False)
-    pend.append(y_send(x_sum(1 - yh, 0, rs1s, rs1r), rs1s, rs1r))
+    sum_third(rs1s, rs1r)
     forward(1 - yl, 1, False)
 
     sent2 = []
@@ -331,7 +396,7 @@
             cp.start()
             sent2.append(cp)
 
-    mixed = y_sum(x_sum(yh, 1, rs1s, rs1r), rs1s, rs1r)
+    mixed = sum_last(rs1s, rs1r)
 
     recip_mix = lax.rsqrt(jnp.mean(mixed * mixed, axis=-1, keepdims=True) + epsilon)
     scaled_mix = mixed * recip_mix
@@ -345,6 +410,7 @@
     g_x[x * 2 + c, 1:2, :] = jnp.sum(cot_f * scaled_mix, axis=0, keepdims=True)
     for cp in pend + sent1:
         cp.wait_send()
+    sum_wait(rs1s, rs1r)
 
     def mz_half(h):
         return (pl.ds(0, B), pl.ds(h * F, F))
@@ -382,6 +448,9 @@
             )
             cp.start()
             sent3.append(cp)
+
+    def z_own(kind, j):
+        buf, _, own, _, _, base = bufs[kind]
         cp = pltpu.make_async_copy(buf.at[j, z], own.at[:, pl.ds(j * T, T)], zl.at[base + j])
         cp.start()
         units[kind, j] = cp
@@ -407,15 +476,11 @@
             remote(ref, ref, hs.at[h * 2 + i], hr.at[h * 2 + i], dev(dz=step[h])).wait_recv()
         mine = shards(z)[h]
         for i in range(2):
-
-            def one(j, _, i=i):
-                cols = pl.ds(pl.multiple_of(h * F + j * T, 128), T)
-                total = nn(ht[ht_rows(mine[i]), :], mgbuf[:, :, :, :, :, cols].reshape(1024, T))
-                total = total + nn(hz[h, i], mzbuf[:, :, :, :, :, cols].reshape(1024, T))
-                zd[h, i, :, tile(j)] = total.astype(bf16)
-                return 0
-
-            lax.fori_loop(0, 3, one, 0)
+            for at, width in ((0, 2 * T), (2 * T, T)):
+                cols = pl.ds(h * F + at, width)
+                total = nn(ht[ht_rows(mine[i]), :], mgbuf[:, :, :, :, :, cols].reshape(1024, width))
+                total = total + nn(hz[h, i], mzbuf[:, :, :, :, :, cols].reshape(1024, width))
+                zd[h, i, :, pl.ds(at, width)] = total.astype(bf16)
         cp = remote(zd.at[h, 1], d_a.at[:, pl.ds(h * F, F)], ds.at[h], dr.at[h], dev(dz=step[1 - h]))
         cp.start()
         sent3.append(cp)
@@ -423,70 +488,79 @@
         cp.start()
         units["d", h] = cp
 
-    def hidden_grad(j):
+    def hidden_grad(j, n):
         def one(k, _):
             a, b = k // 2, k % 2
-            grad = nt(mgbuf[a, b].reshape(256, D), wd[pl.ds(j * T, T), :])
-            cols = pl.ds(j * T, T)
-            act[a, b, :, cols] = (grad * act[a, b, :, cols].astype(f32)).astype(bf16)
-            us[a, b, :, cols] = (grad * us[a, b, :, cols].astype(f32)).astype(bf16)
+            grad = nt(mgbuf[a, b].reshape(256, D), wd[pl.ds(j * T, n * T), :])
+            for i in range(n):
+                part_grad = grad[:, i * T : (i + 1) * T]
+                for m in range(2):
+                    cols = pl.ds(((j + i) * 2 + m) * T, T)
+                    au[a, b, :, cols] = (part_grad * au[a, b, :, cols].astype(f32)).astype(bf16)
             return 0
 
         lax.fori_loop(0, 4, one, 0)
 
-    def in_grad(buf, src, j):
+    def in_grads(j):
         def one(i, _):
-            rhs = src[:, :, :, pl.ds(j * T, T)].reshape(1024, T)
-            lhs = ntr[pl.ds(pl.multiple_of(i * 288, 32), 288), :]
-            buf[j, i] = nn(lhs, rhs).astype(bf16)
+            to = (z + 2 + i) % 4
+            rhs = au[:, :, :, pl.ds(j * 2 * T, 2 * T)].reshape(1024, 2 * T)
+            lhs = ntr[pl.ds(pl.multiple_of(to * 288, 32), 288), :]
+            total = nn(lhs, rhs).astype(bf16)
+            zg[j, to] = total[:, :T]
+            zu[j, to] = total[:, T:]
             return 0
 
-        lax.fori_loop(0, 4, one, 0)
+        lax.fori_loop(0, 1, one, 0)
+        z_first("g", j)
+        z_first("u", j)
+        lax.fori_loop(1, 4, one, 0)
+        z_own("g", j)
+        z_own("u", j)
 
     for h in range(2):
         ref = mzbuf.at[yl, yh, x, c].at[mz_half(h)]
         remote(ref, ref, ms.at[h], mr.at[h], dev(dz=step[h])).wait_recv()
     steps = gather(mzbuf, ag3s, ag3r, sent2)
     next(steps)
-    for j in range(3):
-        hidden_grad(j)
-        next(steps, None)
-        in_grad(zg, us, j)
-        z_first("g", j)
-        next(steps, None)
-        if j >= 1:
-            z_second("g", j - 1)
-        in_grad(zu, act, j)
-        z_first("u", j)
-        next(steps, None)
-        if j >= 1:
-            z_second("u", j - 1)
+    hidden_grad(0, 1)
+    in_grads(0)
+    next(steps)
+    hidden_grad(1, 2)
+    next(steps)
+    in_grads(1)
+    z_second("g", 0)
+    z_second("u", 0)
+    next(steps)
+    in_grads(2)
+    next(steps)
+    z_second("g", 1)
+    z_second("u", 1)
 
     def normed_grad(half):
         def one(j, _):
-            total = nt(us[yl, half], wg[tile(j), :]) + nt(act[yl, half], wu[tile(j), :])
-            part[half, :, :, :, tile(j)] = total.astype(bf16).reshape(4, 2, B, T)
+            total = nt(au[yl, half], wgu[tile(j, 2 * T), :])
+            part[half, :, :, :, tile(j, 2 * T)] = total.astype(bf16).reshape(4, 2, B, 2 * T)
             return 0
 
-        lax.fori_loop(0, 6, one, 0)
+        lax.fori_loop(0, 3, one, 0)
 
     normed_grad(1 - yh)
     pend = [core_send(1 - yh, 0, rs2s, rs2r)]
-    next(steps, None)
+    next(steps)
+    next(steps)
+    z_second("g", 2)
+    z_second("u", 2)
+    sum_first(rs2s, rs2r)
     normed_grad(yh)
     pend.append(core_send(yh, 1, rs2s, rs2r))
-    core_add(1 - yh, 0, rs2s, rs2r)
-    pend += x_send(1 - yh, 0, rs2s, rs2r)
-    next(steps, None)
-    core_add(yh, 1, rs2s, rs2r)
-    pend += x_send(yh, 1, rs2s, rs2r)
-    z_second("g", 2)
+    next(steps)
+    sum_second(rs2s, rs2r)
     run(steps)
     down_grad(0)
-    pend.append(y_send(x_sum(1 - yh, 0, rs2s, rs2r), rs2s, rs2r))
-    z_second("u", 2)
+    sum_third(rs2s, rs2r)
     down_grad(1)
-    grad_in = y_sum(x_sum(yh, 1, rs2s, rs2r), rs2s, rs2r)
+    grad_in = sum_last(rs2s, rs2r)
     tok_f = tok[...].astype(f32)
     recip_in = lax.rsqrt(jnp.mean(tok_f * tok_f, axis=-1, keepdims=True) + epsilon)
     scaled_in = tok_f * recip_in
@@ -534,6 +608,7 @@
         units["d", h].wait()
     for cp in pend + sent2 + sent3:
         cp.wait_send()
+    sum_wait(rs2s, rs2r)
 
 
 def finish(
@@ -565,14 +640,12 @@
         in_specs=[vm] * 4 + [hbm] * 3,
         out_specs=[vm] * 3 + [hbm] * 8,
         scratch_shapes=[
-            V((D, F), bf16),
-            V((D, F), bf16),
+            V((D, 2 * F), bf16),
             V((F, D), bf16),
             V((2, 2, 4, 2, B, D), bf16),
             V((2, 2, 4, 2, B, D), bf16),
             V((2, 2, 4, 2, B, D), bf16),
-            V((2, 2, 256, F), bf16),
-            V((2, 2, 256, F), bf16),
+            V((2, 2, 256, 2 * F), bf16),
             V((2, 256, F), bf16),
             V((F, 1024), bf16),
             V((2, 2, 144, 1024), bf16),
@@ -582,18 +655,17 @@
             V((2, 3, B, D), bf16),
             V((B, D), bf16),
             V((B, D), bf16),
+            V((4, B, D), bf16),
             V((2, 2, 144, F), bf16),
             V((3, 4, 288, T), bf16),
             V((3, 4, 288, T), bf16),
             V((3, 2, 144, T), bf16),
             V((3, 2, 144, T), bf16),
-            V((256, T), f32),
-            V((256, T), f32),
-            V((256, T), f32),
-            V((256, T), f32),
+            V((256, 2 * T), f32),
+            V((256, 2 * T), f32),
             V((8, 2, D), f32),
             V((16, 2, D), f32),
-            dma((3,)),
+            dma((7,)),
             dma((33,)), dma((33,)), dma((32,)), dma((32,)), dma((32,)), dma((32,)),
             dma((9,)), dma((9,)), dma((9,)), dma((9,)),
             dma((24,)), dma((24,)), dma((8,)),
@@ -615,7 +687,7 @@
     def rows(n, width):
         return pl.BlockSpec((n, width), lambda i: (i, 0))
 
-    n = 3
+    n = 1
     return pl.pallas_call(
         finish,
         grid=(n,),

time: 150 us -> 141 us (0.940)
  Pallas kernels: 148 us -> 140 us
    pallas_call x1, Pallas kernels: 143 us -> 135 us  [local(): pl.pallas_call(kernel, out_shape=[S((B, D), bf16), S((B, D), bf16), S((2,...]
where the time goes in v3:
time: 141 us
  Pallas kernels  140 us (99%)
    pallas_call x1, Pallas kernels, local(): pl.pallas_call(kernel, out_shape=[S((B, D), bf16), S((B, D), bf16), S((2,...  135 us
    pallas_call x1, Pallas kernels, local(): pl.pallas_call(finish, grid=(n,), out_shape=[S((B, D), bf16), S((B, D), b...  4.77 us

profile of v3, /device:TPU:1, one launch (start us, length us, event | category | flops | bytes accessed | tf_op | source)
XLA Modules:
  0.0 140.7 jit_solution(11545755710592831701)
XLA Ops:
  0.6 135.2 %shard_map.126 = (bf16[32,2304]{1,0:T(8,128)(2,1)}, bf16[32,2304]{1,0:T(8,128)(2,1)}, f32[2,2304]{1,0:T(2,128)}, bf16[144,2304]{1,0:T(8,128)(2,1)}, bf16[144,230...) custom-call(bf16[32,2304]{1,0:T(8,128)(2,1)} %tok.1, ...), custom_call_target="tpu_custom_call" | custom-call | flops 32999999488 | bytes 30000000 | tf_op jit(solution)/shard_map/pallas_call | solution.py:633
  135.9 4.8 %shard_map.127 = (bf16[32,2304]{1,0:T(8,128)(2,1)}, bf16[32,2304]{1,0:T(8,128)(2,1)}, f32[2304]{0:T(1024)}, f32[2304]{0:T(1024)}, f32[288,1152]{1,0:T(8,128)}, /*index=5*/f32[288,1152]{1,0:T(8,128)}, f32[144,2304]{1,0:T(8,128)}) custom-call(bf16[32,2304]{1,0:T(8,128)(2,1)} %get-tuple-element.18.bout, bf16[32,2304]{1,0:T(8,128)(2,1)} %get-tuple-element.19.tgrad, ...), custom_call_target="tpu_custom_call" | custom-call | tf_op jit(solution)/shard_map/pallas_call | solution.py:691

commit v4 on v3

--- a/solution.py
+++ b/solution.py
@@ -406,8 +406,6 @@
         weighted - scaled_mix * jnp.mean(weighted * scaled_mix, axis=-1, keepdims=True)
     )
     mgbuf[yl, yh, x, c] = mix_grad.astype(bf16)
-    bout[...] = (tok[...].astype(f32) + scaled_mix * gpost).astype(bf16)
-    g_x[x * 2 + c, 1:2, :] = jnp.sum(cot_f * scaled_mix, axis=0, keepdims=True)
     for cp in pend + sent1:
         cp.wait_send()
     sum_wait(rs1s, rs1r)
@@ -421,7 +419,12 @@
         )
         cp.start()
         sent2.append(cp)
-    run(gather(mgbuf, ag2s, ag2r, sent2))
+    steps = gather(mgbuf, ag2s, ag2r, sent2)
+    next(steps)
+    bout[...] = (tok[...].astype(f32) + scaled_mix * gpost).astype(bf16)
+    g_x[x * 2 + c, 1:2, :] = jnp.sum(cot_f * scaled_mix, axis=0, keepdims=True)
+    next(steps)
+    next(steps)
 
     def turn(k, _):
         def one(j, _):
@@ -432,7 +435,10 @@
         lax.fori_loop(0, 3, one, 0)
         return 0
 
-    lax.fori_loop(0, 4, turn, 0)
+    lax.fori_loop(0, 2, turn, 0)
+    next(steps)
+    lax.fori_loop(2, 4, turn, 0)
+    run(steps)
 
     units = {}
     sent3 = []

time: 141 us -> 139 us (0.986)
  no operation moved by 1% of the time
where the time goes in v4:
time: 139 us
  Pallas kernels  139 us (100%)
    pallas_call x1, Pallas kernels, local(): pl.pallas_call(kernel, out_shape=[S((B, D), bf16), S((B, D), bf16), S((2,...  134 us
    pallas_call x1, Pallas kernels, local(): pl.pallas_call(finish, grid=(n,), out_shape=[S((B, D), bf16), S((B, D), b...  4.77 us

profile of v4, /device:TPU:1, one launch (start us, length us, event | category | flops | bytes accessed | tf_op | source)
XLA Modules:
  0.0 139.3 jit_solution(14732078748460235172)
XLA Ops:
  0.6 133.9 %shard_map.126 = (bf16[32,2304]{1,0:T(8,128)(2,1)}, bf16[32,2304]{1,0:T(8,128)(2,1)}, f32[2,2304]{1,0:T(2,128)}, bf16[144,2304]{1,0:T(8,128)(2,1)}, bf16[144,230...) custom-call(bf16[32,2304]{1,0:T(8,128)(2,1)} %tok.1, ...), custom_call_target="tpu_custom_call" | custom-call | flops 32999999488 | bytes 30000000 | tf_op jit(solution)/shard_map/pallas_call | solution.py:639
  134.6 4.8 %shard_map.127 = (bf16[32,2304]{1,0:T(8,128)(2,1)}, bf16[32,2304]{1,0:T(8,128)(2,1)}, f32[2304]{0:T(1024)}, f32[2304]{0:T(1024)}, f32[288,1152]{1,0:T(8,128)}, /*index=5*/f32[288,1152]{1,0:T(8,128)}, f32[144,2304]{1,0:T(8,128)}) custom-call(bf16[32,2304]{1,0:T(8,128)(2,1)} %get-tuple-element.18.bout, bf16[32,2304]{1,0:T(8,128)(2,1)} %get-tuple-element.19.tgrad, ...), custom_call_target="tpu_custom_call" | custom-call | tf_op jit(solution)/shard_map/pallas_call | solution.py:697
